TPU v7x, 128 devices: a whole 4x4x4 slice. The times are simulated.
128 devices in a mesh: row: 16 (over z, x), col: 8 (over y, core).
Axes of the slice: x: 4, y: 4, z: 4, core: 2. Of those that a mesh axis runs over, the one named last changes fastest.
Arguments:
- histograms: bfloat16 [256, 640, 672], P(('row', 'col')), as said below
- basis: bfloat16 [256, 32, 640], P(('row', 'col')), may hold values from -6 to 6
- row_pairs: int32 [128, 16, 2], P(('row', 'col')), may hold values from -1 to 1, as said below
- col_pairs: int32 [128, 8, 2], P(('row', 'col')), may hold values from -1 to 1, as said below
Outputs:
- product: float32 [256, 32, 640], P(('row', 'col'))
Inputs may be any that keep to these rules, and one draw needn't show every extreme that they name: histograms entries are nonnegative. row_pairs[d, s] concerns the device at row s in the column of device d: (own local block, partner local block on that device), or (-1, -1) where device d takes no pair with it, always so at s equal to d's own row; for two devices at most one lists the other, so every pair stands once. col_pairs[d, s] concerns the device at column s in the row of device d, with the same meaning and the same rules.
All inputs are finite; a program needn't handle non-finite values.
Results may differ from a plain program's by a relative error of at most 0.0028.
Values may be sent and summed in bfloat16 or wider, within the bound.
A program may use at most 192 MiB of HBM per device.

v0:
```python
import jax
import jax.numpy as jnp
from jax import lax
from jax.sharding import PartitionSpec as P

F = 672


def kernel_tile(first_rows, second_rows):
    first_sq = jnp.sum(jnp.square(first_rows.astype(jnp.float32)), axis=1)
    second_sq = jnp.sum(jnp.square(second_rows.astype(jnp.float32)), axis=1)
    inner_products = lax.dot_general(
        first_rows, second_rows, (((1,), (1,)), ((), ())), preferred_element_type=jnp.float32
    )
    distances = first_sq[:, None] + second_sq[None, :] - 2.0 * inner_products
    return jnp.exp(-jnp.maximum(distances, 0.0) / (0.09 * F)).astype(jnp.bfloat16)


def pair_terms(histograms, basis, own_index, peer_rows, peer_basis):
    kernel = kernel_tile(histograms[own_index], peer_rows)
    own_part = lax.dot_general(
        peer_basis, kernel, (((1,), (1,)), ((), ())), preferred_element_type=jnp.float32
    )
    peer_part = jnp.dot(basis[own_index], kernel, preferred_element_type=jnp.float32)
    return (own_part, peer_part)


def outgoing(histograms, basis, asked):
    chosen = jnp.maximum(asked, 0)
    present = asked >= 0
    send_rows = jnp.where(present[:, None, None], histograms[chosen], 0)
    send_basis = jnp.where(present[:, None, None], basis[chosen], 0)
    return (send_rows, send_basis)


def pair_slots(table, peer_hist, peer_basis, histograms, basis, product):
    positions = table.shape[0]
    own_block = table[:, 0]
    linked = own_block >= 0
    partials = jnp.zeros((positions,) + basis.shape[1:], jnp.float32)

    def tile_step(position, carry):
        summed, returns = carry
        own_index = jnp.maximum(own_block[position], 0)
        present_flag = linked[position].astype(jnp.float32)
        own_part, peer_part = pair_terms(
            histograms, basis, own_index, peer_hist[position], peer_basis[position]
        )
        summed = summed.at[own_index].add(present_flag * own_part)
        returns = returns.at[position].set(present_flag * peer_part)
        return (summed, returns)

    return lax.fori_loop(0, positions, tile_step, (product, partials))


def credit(returned, asked, own_count):
    selector = (asked[:, None] == jnp.arange(own_count)[None, :]).astype(jnp.float32)
    return jnp.einsum("sb,scr->bcr", selector, returned, precision=lax.Precision.HIGHEST)


def body(histograms, basis, row_pairs, col_pairs):
    own_count = histograms.shape[0]
    row_table = row_pairs[0]
    col_table = col_pairs[0]
    asked_row = lax.all_to_all(row_table[:, 1:2], "row", split_axis=0, concat_axis=0, tiled=True)[
        :, 0
    ]
    asked_col = lax.all_to_all(col_table[:, 1:2], "col", split_axis=0, concat_axis=0, tiled=True)[
        :, 0
    ]
    product = jnp.stack(
        [
            jnp.dot(
                basis[block_id],
                kernel_tile(histograms[block_id], histograms[block_id]),
                preferred_element_type=jnp.float32,
            )
            for block_id in range(own_count)
        ]
    )
    send_rows, send_basis = outgoing(histograms, basis, asked_row)
    peer_hist, peer_basis = (
        lax.all_to_all(send_rows, "row", split_axis=0, concat_axis=0, tiled=True),
        lax.all_to_all(send_basis, "row", split_axis=0, concat_axis=0, tiled=True),
    )
    product, partials = pair_slots(row_table, peer_hist, peer_basis, histograms, basis, product)
    returned = lax.all_to_all(partials, "row", split_axis=0, concat_axis=0, tiled=True)
    product = product + credit(returned, asked_row, own_count)
    send_rows, send_basis = outgoing(histograms, basis, asked_col)
    peer_hist, peer_basis = (
        lax.all_to_all(send_rows, "col", split_axis=0, concat_axis=0, tiled=True),
        lax.all_to_all(send_basis, "col", split_axis=0, concat_axis=0, tiled=True),
    )
    product, col_partials = pair_slots(col_table, peer_hist, peer_basis, histograms, basis, product)
    returned_col = lax.all_to_all(col_partials, "col", split_axis=0, concat_axis=0, tiled=True)
    return product + credit(returned_col, asked_col, own_count)


def solution(mesh):
    in_specs = (
        P(("row", "col"), None, None),
        P(("row", "col"), None, None),
        P(("row", "col"), None, None),
        P(("row", "col"), None, None),
    )
    out_specs = P(("row", "col"), None, None)
    return jax.shard_map(body, mesh=mesh, in_specs=in_specs, out_specs=out_specs, check_vma=False)
```

profile of v0, /device:TPU:0, one launch (start us, length us, event | category | flops | bytes accessed | tf_op | source)
XLA Modules:
  0.0 726.6 jit_solution(12213443168443273600)
XLA Ops:
  1.4 8.0 %all-to-all-start = ((s32[16,1,1]{2,1,0:T(1,128)}), s32[16,1,1]{2,1,0:T(1,128)S(1)}, u32[]{:S(2)}, u32[]{:S(2)}) async-start(s32[16,1,1]{2,1,0:T(1,128)} %copy.39), calls=%async_computation | async-start | bytes 16384 | tf_op jit(solution)/shard_map/all_to_all | solution.py:65
  10.8 6.1 all-to-all-done
  16.9 4.5 all-to-all-start.4
  22.1 8.3 %gather_fusion.1 = bf16[16,640,672]{1,2,0:T(8,128)(2,1)} fusion(bf16[2,640,672]{1,2,0:T(8,128)(2,1)} %param.16, s32[1024]{0:T(1024)S(1)} %pad_clamp_fusion.1), kind=kCustom, calls=%fused_computation.1 | custom fusion | bytes 27525184 | tf_op jit(solution)/shard_map/gather | solution.py:31
  32.4 3.6 all-to-all-start.1
  36.0 13.0 %broadcast_select_fusion = bf16[16,640,672]{1,2,0:T(8,128)(2,1)} fusion(bf16[16,640,672]{1,2,0:T(8,128)(2,1)} %gather_fusion.1, pred[16]{0:T(512)(128)(4,1)S(1)} %compare_reduce_fusion), kind=kLoop, calls=%fused_computation.62 | loop fusion | flops 6881280 | bytes 27525136 | tf_op jit(solution)/shard_map/jit(_where)/select_n | solution.py:31
  51.1 6.0 all-to-all-start.2
  62.2 201.6 %all-to-all-done.2 = bf16[16,640,672]{1,2,0:T(8,128)(2,1)} async-done(((bf16[16,640,672]{1,2,0:T(8,128)(2,1)}), bf16[16,640,672]{1,2,0:T(8,128)(2,1)}, u32[]{:S(2)}, u32[]{:S(2)}) %all-to-all-start.2) | async-done | bytes 13762592 | tf_op jit(solution)/shard_map/all_to_all | solution.py:83
  263.7 3.4 all-to-all-start.5
  268.4 226.2 %while.34 = (s32[]{:T(128)}, f32[2,32,640]{2,1,0:T(8,128)S(1)}, f32[16,32,640]{2,1,0:T(8,128)}, s32[16]{0:T(128)S(1)}, pred[16]{0:T(512)(128)(4,1)S(1)}, /*index...) while((s32[]{:T(128)}, f32[2,32,640]{2,1,0:T(8,128)S(1)}, ...), condition=%wide.region_7.8_spmd, body=%wide.region_2.7_spmd.sunk | while | flops 608480064 | bytes 9766098 | solution.py:53
  278.3 2.5 fusion.110
  292.4 2.5 fusion.110
  306.6 2.5 fusion.110
  320.7 2.5 fusion.110
  334.8 2.5 fusion.110
  349.0 2.5 fusion.110
  363.1 2.5 fusion.110
  377.2 2.5 fusion.110
  391.4 2.5 fusion.110
  419.7 2.5 fusion.110
  433.8 2.5 fusion.110
  447.9 2.5 fusion.110
  476.2 2.5 fusion.110
  494.6 4.4 all-to-all-start.3
  499.0 4.3 gather_fusion.3
  503.3 6.5 broadcast_select_fusion.1
  509.8 13.0 %all-to-all-done.3 = f32[16,32,640]{2,1,0:T(8,128)} async-done(((f32[16,32,640]{2,1,0:T(8,128)}), f32[16,32,640]{2,1,0:T(8,128)}, u32[]{:S(2)}, u32[]{:S(2)}) %all-to-all-start.3) | async-done | bytes 1310752 | tf_op jit(solution)/shard_map/all_to_all | solution.py:87
  522.7 5.0 all-to-all-start.6
  527.8 2.6 fusion.38
  531.0 75.0 %all-to-all-done.6 = bf16[8,640,672]{1,2,0:T(8,128)(2,1)} async-done(((bf16[8,640,672]{1,2,0:T(8,128)(2,1)}), bf16[8,640,672]{1,2,0:T(8,128)(2,1)}, u32[]{:S(2)}, u32[]{:S(2)}) %all-to-all-start.6) | async-done | bytes 6881312 | tf_op jit(solution)/shard_map/all_to_all | solution.py:91
  606.1 104.8 %while.35 = (s32[]{:T(128)}, f32[2,32,640]{2,1,0:T(8,128)}, f32[8,32,640]{2,1,0:T(8,128)S(1)}, s32[8]{0:T(128)S(1)}, pred[8]{0:T(512)(128)(4,1)S(1)}, /*index=5*...) while((s32[]{:T(128)}, f32[2,32,640]{2,1,0:T(8,128)}, ...), condition=%wide.region_13.14_spmd, body=%wide.region_8.13_spmd.sunk | while | flops 608480064 | bytes 11074839 | solution.py:53
  710.8 14.3 %all_to_all.48 = f32[8,32,640]{2,1,0:T(8,128)S(1)} all-to-all(f32[8,32,640]{2,1,0:T(8,128)S(1)} %get-tuple-element.406), channel_id=1, replica_groups=mesh['row'=16,'col'=8] {'col'}, dimensions={0} | all-to-all | bytes 1310720 | tf_op jit(solution)/shard_map/all_to_all | solution.py:95
  (307 shorter events, 283.1 us)
Async XLA Ops:
  1.4 15.4 %all-to-all-start = ((s32[16,1,1]{2,1,0:T(1,128)}), s32[16,1,1]{2,1,0:T(1,128)S(1)}, u32[]{:S(2)}, u32[]{:S(2)}) async-start(s32[16,1,1]{2,1,0:T(1,128)} %copy.39), calls=%async_computation | async-start | bytes 16384 | tf_op jit(solution)/shard_map/all_to_all | solution.py:65
  16.9 15.5 %all-to-all-start.4 = ((s32[8,1,1]{2,1,0:T(1,128)}), s32[8,1,1]{2,1,0:T(1,128)S(1)}, u32[]{:S(2)}, u32[]{:S(2)}) async-start(s32[8,1,1]{2,1,0:T(1,128)} %copy.43), calls=%async_computation.4 | async-start | bytes 8192 | tf_op jit(solution)/shard_map/all_to_all | solution.py:68
  22.0 8.3 %copy-start.1 = (bf16[2,32,640]{2,1,0:T(8,128)(2,1)S(1)}, bf16[2,32,640]{2,1,0:T(8,128)(2,1)}, u32[]{:S(2)}) copy-start(bf16[2,32,640]{2,1,0:T(8,128)(2,1)} %param.17) | copy-start | bytes 245764
  32.4 17.9 %all-to-all-start.1 = ((bf16[16,32,640]{2,1,0:T(8,128)(2,1)}), bf16[16,32,640]{2,1,0:T(8,128)(2,1)S(1)}, u32[]{:S(2)}, u32[]{:S(2)}) async-start(bf16[16,32,640]{2,1,0:T(8,128)(2,1)} %broadcast_select_fusion.2), calls=%async_computation.1 | async-start | bytes 1310720 | tf_op jit(solution)/shard_map/all_to_all | solution.py:84
  49.0 8.0 %copy-start = (bf16[2,640,672]{1,2,0:T(8,128)(2,1)S(1)}, bf16[2,640,672]{1,2,0:T(8,128)(2,1)}, u32[]{:S(2)}) copy-start(bf16[2,640,672]{1,2,0:T(8,128)(2,1)} %param.16) | copy-start | bytes 5160964
  50.2 0.8 copy-start.5
  51.1 212.7 %all-to-all-start.2 = ((bf16[16,640,672]{1,2,0:T(8,128)(2,1)}), bf16[16,640,672]{1,2,0:T(8,128)(2,1)}, u32[]{:S(2)}, u32[]{:S(2)}) async-start(bf16[16,640,672]{1,2,0:T(8,128)(2,1)} %broadcast_select_fusion), calls=%async_computation.2 | async-start | bytes 27525120 | tf_op jit(solution)/shard_map/all_to_all | solution.py:83
  58.7 1.3 copy-start.10
  60.5 207.9 %copy-start.7 = (s32[3]{0:T(128)S(1)}, s32[3]{0:T(128)}, u32[]{:S(2)}) copy-start(s32[3]{0:T(128)} %constant.253.clone.1) | copy-start | bytes 40
  60.5 207.9 %copy-start.9 = (s32[3]{0:T(128)S(1)}, s32[3]{0:T(128)}, u32[]{:S(2)}) copy-start(s32[3]{0:T(128)} %constant.258.clone.1) | copy-start | bytes 40
  263.7 230.8 %all-to-all-start.5 = ((bf16[8,32,640]{2,1,0:T(8,128)(2,1)}), bf16[8,32,640]{2,1,0:T(8,128)(2,1)S(1)}, u32[]{:S(2)}, u32[]{:S(2)}) async-start(bf16[8,32,640]{2,1,0:T(8,128)(2,1)} %broadcast_select_fusion.3), calls=%async_computation.5 | async-start | bytes 655360 | tf_op jit(solution)/shard_map/all_to_all | solution.py:92
  494.6 8.7 %copy-start.6 = (bf16[8,32,640]{2,1,0:T(8,128)(2,1)}, bf16[8,32,640]{2,1,0:T(8,128)(2,1)S(1)}, u32[]{:S(2)}) copy-start(bf16[8,32,640]{2,1,0:T(8,128)(2,1)S(1)} %all-to-all-done.5) | copy-start | bytes 983044
  494.6 28.1 %all-to-all-start.3 = ((f32[16,32,640]{2,1,0:T(8,128)}), f32[16,32,640]{2,1,0:T(8,128)}, u32[]{:S(2)}, u32[]{:S(2)}) async-start(f32[16,32,640]{2,1,0:T(8,128)} %get-tuple-element.404), calls=%async_computation.3 | async-start | bytes 2621440 | tf_op jit(solution)/shard_map/all_to_all | solution.py:87
  509.8 18.0 %copy-start.11 = (s32[1,8,2]{1,2,0:T(2,128)S(1)}, s32[1,8,2]{1,2,0:T(2,128)}, u32[]{:S(2)}) copy-start(s32[1,8,2]{1,2,0:T(2,128)} %param.19) | copy-start | bytes 196
  522.7 83.3 %all-to-all-start.6 = ((bf16[8,640,672]{1,2,0:T(8,128)(2,1)}), bf16[8,640,672]{1,2,0:T(8,128)(2,1)}, u32[]{:S(2)}, u32[]{:S(2)}) async-start(bf16[8,640,672]{1,2,0:T(8,128)(2,1)} %broadcast_select_fusion.1), calls=%async_computation.6 | async-start | bytes 13762560 | tf_op jit(solution)/shard_map/all_to_all | solution.py:91
  527.7 78.3 %copy-start.8 = (s32[3]{0:T(128)S(1)}, s32[3]{0:T(128)}, u32[]{:S(2)}) copy-start(s32[3]{0:T(128)} %constant.268.clone.1) | copy-start | bytes 40
  611.5 5.3 copy-start.2
  618.5 0.7 copy-start.3
  624.6 5.3 copy-start.2
  631.6 0.7 copy-start.3
  637.7 5.3 copy-start.2
  650.8 5.3 copy-start.2
  657.8 0.7 copy-start.3
  663.9 5.3 copy-start.2
  670.9 0.7 copy-start.3
  677.0 5.3 copy-start.2
  684.0 0.7 copy-start.3
  690.1 5.3 copy-start.2
  697.1 0.7 copy-start.3
  703.2 5.3 copy-start.2
  710.1 0.7 copy-start.3
  710.8 15.1 %copy-start.4 = (f32[2,32,640]{2,1,0:T(8,128)S(1)}, f32[2,32,640]{2,1,0:T(8,128)}, u32[]{:S(2)}) copy-start(f32[2,32,640]{2,1,0:T(8,128)} %get-tuple-element.405) | copy-start | bytes 491524
  (1 other events, 0.7 us)
where the time goes:
time: 734 us; the launch traced here: 727 us
  waiting for transfers between devices  297 us (40%)
  matrix products  149 us (20%)
  local copies, waits for them, and re-layouts  145 us (20%)
  other arithmetic  54.9 us (7%)
  starting transfers between devices  34.8 us (5%)
  loops' own time  31.7 us (4%)
  blocking collectives  14.3 us (2%)
    all_to_all x1, waiting for transfers between devices, body(): lax.all_to_all(send_rows, 'row', split_axis=0, concat_axis=0, tiled=True)  202 us
    dynamic_slice x48, local copies, waits for them, and re-layouts, tile_step(): peer_hist[position]  89.3 us
    all_to_all x1, waiting for transfers between devices, body(): lax.all_to_all(send_rows, 'col', split_axis=0, concat_axis=0, tiled=True)  75 us
    dot_general x24, matrix products, kernel_tile(): lax.dot_general(first_rows, second_rows, (((1,), (1,)), ((), ())), prefer...  54.3 us
    dot_general x24, matrix products, pair_terms(): jnp.dot(basis[own_index], kernel, preferred_element_type=jnp.float32)  46.9 us
    dot_general x24, matrix products, pair_terms(): lax.dot_general(peer_basis, kernel, (((1,), (1,)), ((), ())), preferred_e...  42.1 us
    another operation x2, loops' own time, pair_slots(): return lax.fori_loop(0, positions, tile_step, (product, partials))  31.7 us
    select_n x2, other arithmetic, outgoing(): send_rows = jnp.where(present[:, None, None], histograms[chosen], 0)  19.5 us
  transfers between devices with their start and end apart: 7, of which 5 were waited for; matrix products, arithmetic and copies ran while one was open for 34% of the time, Pallas kernels for 0%

commit v1 on v0

v1 whole, which is shorter than its diff:
```python
import jax
import jax.numpy as jnp
from jax import lax
from jax.experimental import pallas as pl
from jax.experimental.pallas import tpu as pltpu
from jax.sharding import PartitionSpec as P

F = 672
BS = 640
COLS = 32
MAIN = 640
WIDE = 768
SCALE = 1.4426950408889634 / (0.09 * F)
MESH = pl.DeviceIdType.MESH
NT = (((1,), (1,)), ((), ()))
F32 = jnp.float32
BF16 = jnp.bfloat16

OWN, X1, X2, Z1, Z2, Y1, Y2, SIB, DG = range(9)
TAB_Z, TAB_X = 9, 10
SLOTS = 9
M0, M1, SIDE, SQ, TAB, SIDE_B = range(6)

STEPS0 = [(0, 0), (0, 0), (0, 0), (0, 1), (0, 3), (1, 3), (0, 5), (7, 5), (0, 0), (7, 6), (0, 6), (1, 4), (2, 3), (0, 2), (0, 4), (0, 8)]
STEPS1 = [(0, 0), (0, 0), (0, 7), (0, 1), (0, 3), (1, 3), (0, 5), (7, 5), (0, 0), (0, 0), (0, 6), (1, 4), (2, 3), (0, 2), (0, 4), (0, 8)]
COL_STEPS = (2, 6, 7, 9, 10)
N_STEPS = 16


def pick(index, values):
    result = values[-1]
    for position in range(len(values) - 2, -1, -1):
        result = jnp.where(index == position, values[position], result)
    return result


def item_kernel(hist, basis, row_table, col_table, out, H, X, S, Q, T, QC, BR, ACC, RET, STA, STB,
                in_sem, send_sem, recv_sem, back_send, back_recv):
    r = lax.axis_index("row")
    c = lax.axis_index("col")
    z, x, y, k = r // 4, lax.rem(r, 4), c // 2, lax.rem(c, 2)
    s = 1 - 2 * k

    def row_at(dx, dz):
        return lax.rem(z + s * dz + 8, 4) * 4 + lax.rem(x + s * dx + 8, 4)

    def col_at(dy):
        return lax.rem(y + s * dy + 8, 4) * 2 + k

    def on_row(dx, dz):
        return (row_at(dx, dz), c)

    def on_col(dy):
        return (r, col_at(dy))

    sibling = (r, y * 2 + 1 - k)
    cross = (r, lax.rem(y + s + 4, 4) * 2 + 1 - k)
    sib_owner_col = jnp.where(k == 0, cross[1], sibling[1])

    peers = [on_row(1, 0), on_row(-1, 0), on_row(2, 0), on_row(0, 1), on_row(0, -1), on_row(0, 2),
             on_row(1, 1), on_row(-1, -1), on_col(1), on_col(-1), on_col(2), sibling, cross]
    barrier = pltpu.get_barrier_semaphore()
    for peer in peers:
        pl.semaphore_signal(barrier, inc=1, device_id=peer, device_id_type=MESH)

    def copies_in(b):
        return [pltpu.make_async_copy(hist.at[b], H.at[b], in_sem.at[b]),
                pltpu.make_async_copy(hist.at[b, :, pl.ds(0, MAIN)], X.at[OWN, b, :, pl.ds(0, MAIN)], in_sem.at[2 + b])]

    for b in range(2):
        for item in copies_in(b):
            item.start()

    ACC[...] = jnp.zeros_like(ACC)

    def load_table(i, carry):
        T[OWN, 2 * i] = row_table[0, i, 0]
        T[OWN, 2 * i + 1] = row_table[0, i, 1]
        return carry

    lax.fori_loop(0, 16, load_table, 0)

    def load_col(i, carry):
        T[OWN, 32 + 2 * i] = col_table[0, i, 0]
        T[OWN, 33 + 2 * i] = col_table[0, i, 1]
        return carry

    lax.fori_loop(0, 8, load_col, 0)

    lane = lax.broadcasted_iota(jnp.int32, (BS, 128), 1)
    low = lane < 32

    BR[OWN] = basis[...]
    basis_cols = jnp.concatenate([jnp.zeros((64, BS), F32), basis[0].astype(F32), basis[1].astype(F32)], axis=0).T
    for b in range(2):
        for item in copies_in(b):
            item.wait()
        X[OWN, b, :, MAIN:WIDE] = jnp.zeros((BS, 128), BF16)
        X[OWN, b, :, MAIN:F] = H[b, :, MAIN:F]
    tails = [X[OWN, b, :, MAIN:WIDE].astype(F32) for b in range(2)]
    S[OWN] = (basis_cols + tails[0] + pltpu.roll(tails[1], 32, 1)).astype(BF16)
    for b in range(2):
        values = X[OWN, b].astype(F32)
        column = jnp.sum(values * values, axis=1, keepdims=True) * (-SCALE)
        QC[OWN, b] = column
        Q[OWN, b:b + 1] = jnp.broadcast_to(column, (BS, 128)).T[0:1]

    pl.semaphore_wait(barrier, len(peers))

    def remote(src, dst, send, recv, device):
        return pltpu.make_async_remote_copy(src_ref=src, dst_ref=dst, send_sem=send, recv_sem=recv,
                                            device_id=device, device_id_type=MESH)

    def part(kind, slot):
        if kind in (M0, M1):
            return X.at[slot, kind, :, pl.ds(0, MAIN)]
        return {SIDE: S, SQ: Q, TAB: T}[kind].at[slot]

    def copy(path, kind, src, dst, device):
        return remote(part(kind, src), part(kind, dst), send_sem.at[path, kind], recv_sem.at[dst, kind], device)

    def arrived(kind, slot):
        copy(0, kind, slot, slot, sibling).wait_recv()

    paths = [(0, OWN, X1, on_row(1, 0)), (1, OWN, Z1, on_row(0, 1)), (2, OWN, Y1, on_col(1)),
             (4, X1, X2, on_row(1, 0)), (5, Z1, Z2, on_row(0, 1)), (6, Y1, Y2, on_col(1))]
    small = (TAB, SQ, SIDE)

    for kind in (TAB, SQ, SIDE, M0, M1):
        for path in paths[:3]:
            copy(path[0], kind, *path[1:]).start()
        if kind == TAB:
            copy(9, TAB, OWN, TAB_Z, on_row(0, -1)).start()
            copy(10, TAB, OWN, TAB_X, on_row(-1, 0)).start()

        @pl.when(k == 0)
        def _():
            copy(3, kind, OWN, SIB, sibling).start()

    def prepare(slot, as_left):
        side = S[slot].astype(F32)
        X[slot, 0, :, MAIN:WIDE] = jnp.where(low, side, 0.0).astype(BF16)
        X[slot, 1, :, MAIN:WIDE] = jnp.where(low, pltpu.roll(side, 96, 1), 0.0).astype(BF16)
        if as_left:
            rows = side.T
            BR[slot, 0] = rows[64:96].astype(BF16)
            BR[slot, 1] = rows[96:128].astype(BF16)
            columns = Q[slot].T
            QC[slot, 0] = columns[:, 0:1]
            QC[slot, 1] = columns[:, 1:2]

    def row_of(slot):
        return pick(slot, [r, row_at(-1, 0), row_at(-2, 0), row_at(0, -1), row_at(0, -2), r, r, r, row_at(-1, -1)])

    def col_of(slot):
        return pick(slot, [c, c, c, c, c, col_at(-1), col_at(-2), sib_owner_col, c])

    def chosen(i, j, ki, kj):
        return jnp.maximum(T[i, kj], T[j, ki + 1]), jnp.maximum(T[i, kj + 1], T[j, ki])

    def stage_a():
        target, owner = 2 * row_at(0, 1), 2 * row_at(-1, 0)
        return jnp.maximum(T[X1, target], T[TAB_Z, owner + 1])

    def stage_b():
        target, owner = 2 * row_at(1, 0), 2 * row_at(0, -1)
        return jnp.maximum(T[Z1, target], T[TAB_X, owner + 1])

    first, second = pl.ds(0, BS // 2), pl.ds(BS // 2, BS // 2)
    to_z, to_x = on_row(0, 1), on_row(1, 0)

    def diagonal_copies():
        return [
            remote(STA, X.at[DG, 0, first, pl.ds(0, MAIN)], send_sem.at[7, M0], recv_sem.at[DG, M0], to_z),
            remote(S.at[X1, first], S.at[DG, first], send_sem.at[7, SIDE], recv_sem.at[DG, SIDE], to_z),
            copy(7, SQ, X1, DG, to_z),
            copy(7, TAB, X1, DG, to_z),
            remote(STB, X.at[DG, 0, second, pl.ds(0, MAIN)], send_sem.at[8, M1], recv_sem.at[DG, M1], to_x),
            remote(S.at[Z1, second], S.at[DG, second], send_sem.at[8, SIDE], recv_sem.at[DG, SIDE_B], to_x),
        ]

    owners = [None, on_row(-1, 0), on_row(-2, 0), on_row(0, -1), on_row(0, -2), on_col(-1), on_col(-2),
              (r, sib_owner_col), on_row(-1, -1)]

    def give_back(slot):
        return remote(ACC.at[slot], RET.at[slot - 1], back_send.at[slot - 1], back_recv.at[slot - 1], owners[slot])

    def step_body(step, carry):
        @pl.when(jnp.logical_and(step == 2, k == 1))
        def _():
            for kind in (TAB, SQ, SIDE, M0, M1):
                arrived(kind, SIB)
            prepare(SIB, True)

        @pl.when(step == 3)
        def _():
            for slot in (X1, Z1, Y1):
                for kind in small:
                    arrived(kind, slot)
            arrived(TAB, TAB_Z)
            arrived(TAB, TAB_X)
            for kind in small:
                for path in paths[3:]:
                    copy(path[0], kind, *path[1:]).start()

                @pl.when(k == 1)
                def _():
                    copy(3, kind, Y1, SIB, sibling).start()
            for slot in (X1, Z1, Y1):
                prepare(slot, slot == X1)
            for kind in (M0, M1):
                for slot, path in zip((X1, Z1, Y1), paths[3:]):
                    arrived(kind, slot)
                    copy(path[0], kind, *path[1:]).start()

                @pl.when(k == 1)
                def _():
                    copy(3, kind, Y1, SIB, sibling).start()

        @pl.when(jnp.logical_and(step == 7, k == 0))
        def _():
            for kind in (TAB, SQ, SIDE, M0, M1):
                arrived(kind, SIB)
            prepare(SIB, True)

        @pl.when(step == 8)
        def _():
            STA[...] = jnp.where(stage_a() == 0, X[X1, 0, 0:BS // 2, 0:MAIN], X[X1, 1, 0:BS // 2, 0:MAIN])
            STB[...] = jnp.where(stage_b() == 0, X[Z1, 0, BS // 2:BS, 0:MAIN], X[Z1, 1, BS // 2:BS, 0:MAIN])
            for item in diagonal_copies():
                item.start()

        @pl.when(step == 9)
        def _():
            for kind in (TAB, SQ, SIDE, M0, M1):
                arrived(kind, Y2)
            prepare(Y2, False)

        @pl.when(step == 11)
        def _():
            for slot in (Y1, Y2, SIB):
                give_back(slot).start()
            for slot in (X2, Z2):
                for kind in (TAB, SQ, SIDE, M0, M1):
                    arrived(kind, slot)
                prepare(slot, slot == X2)

        @pl.when(step == 15)
        def _():
            for slot in (X1, X2, Z1, Z2):
                give_back(slot).start()
            for item in diagonal_copies():
                item.wait_recv()
            side = S[DG].astype(F32)
            own_key, their_key = 2 * r, 2 * row_at(-1, -1)
            theirs = jnp.maximum(T[OWN, their_key + 1], T[DG, own_key])
            tail = jnp.where(theirs == 0, side, pltpu.roll(side, 96, 1))
            X[DG, 0, :, MAIN:WIDE] = jnp.where(low, tail, 0.0).astype(BF16)

        i = pick(step, [jnp.where(k == 0, a[0], b[0]) if a != b else a[0] for a, b in zip(STEPS0, STEPS1)])
        j = pick(step, [jnp.where(k == 0, a[1], b[1]) if a != b else a[1] for a, b in zip(STEPS0, STEPS1)])
        west = x < 2
        i = jnp.where(jnp.logical_and(step == 13, jnp.logical_not(west)), X2, i)
        j = jnp.where(jnp.logical_and(step == 13, jnp.logical_not(west)), Z2, j)
        runs = step != 8
        runs = jnp.logical_and(runs, jnp.logical_or(step != 2, k == 1))
        runs = jnp.logical_and(runs, jnp.logical_or(step != 9, k == 0))
        runs = jnp.logical_and(runs, jnp.logical_or(step != 10, y < 2))
        runs = jnp.logical_and(runs, jnp.logical_or(step != 14, z < 2))

        @pl.when(runs)
        def _():
            along_col = step == COL_STEPS[0]
            for other in COL_STEPS[1:]:
                along_col = jnp.logical_or(along_col, step == other)
            ki = jnp.where(along_col, 32 + 2 * col_of(i), 2 * row_of(i))
            kj = jnp.where(along_col, 32 + 2 * col_of(j), 2 * row_of(j))
            bi, bj = chosen(i, j, ki, kj)
            diagonal = step < 2
            bi = jnp.where(diagonal, step, bi)
            bj = jnp.where(diagonal, step, bj)
            at = jnp.where(j == DG, 0, bj)
            left = jnp.where(bi == 0, X[i, 0], X[i, 1])
            right = jnp.where(at == 0, X[j, 0], X[j, 1])
            inner = lax.dot_general(left, right, NT, preferred_element_type=F32)
            squares = jnp.where(bi == 0, QC[i, 0], QC[i, 1]) + jnp.where(bj == 0, Q[j, 0:1], Q[j, 1:2])
            kernel = jnp.exp2(jnp.minimum(inner * (2 * SCALE) + squares, 0.0)).astype(BF16)
            theirs = jnp.dot(kernel, S[j], preferred_element_type=F32).T
            theirs = jnp.where(bj == 0, theirs[64:96], theirs[96:128])
            mine = jnp.dot(jnp.where(bi == 0, BR[i, 0], BR[i, 1]), kernel, preferred_element_type=F32)
            for b in range(2):
                ACC[i, b] += jnp.where(jnp.logical_and(bi == b, jnp.logical_not(diagonal)), theirs, 0.0)
                ACC[j, b] += jnp.where(bj == b, mine, 0.0)

        return carry

    lax.fori_loop(0, N_STEPS, step_body, 0)
    give_back(DG).start()

    for path in paths:
        for kind in (TAB, SQ, SIDE, M0, M1):
            copy(path[0], kind, *path[1:]).wait_send()
    for kind in (TAB, SQ, SIDE, M0, M1):
        copy(3, kind, OWN, SIB, sibling).wait_send()
    copy(9, TAB, OWN, TAB_Z, on_row(0, -1)).wait_send()
    copy(10, TAB, OWN, TAB_X, on_row(-1, 0)).wait_send()
    for item in diagonal_copies():
        item.wait_send()
    total = ACC[OWN]
    for slot in (Y1, Y2, SIB, X1, X2, Z1, Z2, DG):
        give_back(slot).wait()
        total = total + RET[slot - 1]
    out[...] = total


def body(histograms, basis, row_pairs, col_pairs):
    return pl.pallas_call(
        item_kernel,
        out_shape=jax.ShapeDtypeStruct((2, COLS, BS), F32),
        in_specs=[
            pl.BlockSpec(memory_space=pl.ANY),
            pl.BlockSpec(memory_space=pltpu.VMEM),
            pl.BlockSpec(memory_space=pltpu.SMEM),
            pl.BlockSpec(memory_space=pltpu.SMEM),
        ],
        out_specs=pl.BlockSpec(memory_space=pltpu.VMEM),
        scratch_shapes=[
            pltpu.VMEM((2, BS, F), BF16),
            pltpu.VMEM((SLOTS, 2, BS, WIDE), BF16),
            pltpu.VMEM((SLOTS, BS, 128), BF16),
            pltpu.VMEM((SLOTS, 8, BS), F32),
            pltpu.SMEM((11, 48), jnp.int32),
            pltpu.VMEM((SLOTS, 2, BS, 1), F32),
            pltpu.VMEM((SLOTS, 2, COLS, BS), BF16),
            pltpu.VMEM((SLOTS, 2, COLS, BS), F32),
            pltpu.VMEM((SLOTS - 1, 2, COLS, BS), F32),
            pltpu.VMEM((BS // 2, MAIN), BF16),
            pltpu.VMEM((BS // 2, MAIN), BF16),
            pltpu.SemaphoreType.DMA((4,)),
            pltpu.SemaphoreType.DMA((11, 5)),
            pltpu.SemaphoreType.DMA((11, 6)),
            pltpu.SemaphoreType.DMA((SLOTS - 1,)),
            pltpu.SemaphoreType.DMA((SLOTS - 1,)),
        ],
        compiler_params=pltpu.CompilerParams(
            collective_id=0, has_side_effects=True, vmem_limit_bytes=56 * 1024 * 1024
        ),
    )(histograms, basis, row_pairs, col_pairs)


def solution(mesh):
    spec = P(("row", "col"), None, None)
    return jax.shard_map(body, mesh=mesh, in_specs=(spec,) * 4, out_specs=spec, check_vma=False)
```

time: 734 us -> 78.3 us (0.11)
  waiting for transfers between devices: 297 us -> 0 us
  matrix products: 149 us -> 0 us
  local copies, waits for them, and re-layouts: 145 us -> 8.12 us
  Pallas kernels: 0 us -> 69.9 us
  other arithmetic: 54.9 us -> 0 us
  starting transfers between devices: 34.8 us -> 0 us
  loops' own time: 31.7 us -> 0 us
  blocking collectives: 14.3 us -> 0 us
    all_to_all x7 -> x0, waiting for transfers between devices: 297 us -> none  [the longest x1 202 us: body(): lax.all_to_all(send_rows, 'row', split_axis=0, concat_axis=0, tiled=True)]
    dot_general x76 -> x0, matrix products: 149 us -> none  [the longest x24 54.3 us: kernel_tile(): lax.dot_general(first_rows, second_rows, (((1,), (1,)), ((), ())), prefer...]
    dynamic_slice x96 -> x0, local copies, waits for them, and re-layouts: 120 us -> none  [the longest x48 89.3 us: tile_step(): peer_hist[position]]
    pallas_call x0 -> x1, Pallas kernels: none -> 69.9 us  [body(): pl.pallas_call(item_kernel, out_shape=jax.ShapeDtypeStruct((2, COLS, BS),...]
    all_to_all x7 -> x0, starting transfers between devices: 34.8 us -> none  [the longest x1 7.96 us: body(): lax.all_to_all(row_table[:, 1:2], 'row', split_axis=0, concat_axis=0, til...]
    another operation x2 -> x0, loops' own time: 31.7 us -> none  [pair_slots(): return lax.fori_loop(0, positions, tile_step, (product, partials))]
    select_n x4 -> x0, other arithmetic: 21.3 us -> none  [the longest x2 19.5 us: outgoing(): send_rows = jnp.where(present[:, None, None], histograms[chosen], 0)]
    another operation x25 -> x0, other arithmetic: 18.9 us -> none
  transfers between devices with their start and end apart: 7 -> 0, of which waited for: 5 -> 0; matrix products, arithmetic and copies ran while one was open for 34% -> 0% of each run, Pallas kernels for 0% -> 0%
where the time goes in v1:
time: 78.3 us; the launch traced here: 78 us
  Pallas kernels  69.9 us (89%)
  local copies, waits for them, and re-layouts  8.12 us (10%)
    pallas_call x1, Pallas kernels, body(): pl.pallas_call(item_kernel, out_shape=jax.ShapeDtypeStruct((2, COLS, BS),...  69.9 us
    unnamed x4, local copies, waits for them, and re-layouts  8.12 us

profile of v1, /device:TPU:0, one launch (start us, length us, event | category | flops | bytes accessed | tf_op | source)
XLA Modules:
  0.0 78.0 jit_solution(9489628881459682706)
XLA Ops:
  0.0 1.3 %copy.7.col_table = s32[1,8,2]{2,1,0:T(8,128)} copy(s32[1,8,2]{1,2,0:T(2,128)} %param.7) | data formatting | bytes 128 | tf_op args[3]
  1.3 1.4 %copy.6.row_table = s32[1,16,2]{2,1,0:T(8,128)} copy(s32[1,16,2]{1,2,0:T(2,128)} %param.6) | data formatting | bytes 256 | tf_op args[2]
  2.7 3.8 %copy.5.hist = bf16[2,640,672]{2,1,0:T(8,128)(2,1)} copy(bf16[2,640,672]{1,2,0:T(8,128)(2,1)} %param.4) | data formatting | bytes 3440640 | tf_op args[0]
  6.5 69.9 %shard_map.46 = f32[2,32,640]{2,1,0:T(8,128)} custom-call(bf16[2,640,672]{2,1,0:T(8,128)(2,1)} %copy.5.hist, bf16[2,32,640]{2,1,0:T(8,128)(2,1)} %basis.1, s32[1,16,2]{2,1,0:T(8,128)} %copy.6.row_table, s32[1,8,2]{2,1,0:T(8,128)} %copy.7.col_table), custom_call_target="tpu_custom_call" | custom-call | tf_op jit(solution)/shard_map/pallas_call | solution.py:317
  76.4 1.6 %copy.9 = f32[2,32,640]{2,1,0:T(8,128)} copy(f32[2,32,640]{2,1,0:T(8,128)} %shard_map.46) | data formatting | bytes 327680

commit v2 on v1

v2 whole, which is shorter than its diff:
```python
import jax
import jax.numpy as jnp
from jax import lax
from jax.experimental import pallas as pl
from jax.experimental.pallas import tpu as pltpu
from jax.sharding import PartitionSpec as P

F = 672
BS = 640
COLS = 32
SCALE = 1.4426950408889634 / (0.09 * F)
MESH = pl.DeviceIdType.MESH
NT = (((1,), (1,)), ((), ()))
TN = (((0,), (0,)), ((), ()))
F32 = jnp.float32
BF16 = jnp.bfloat16

OWN, X1, X2, Z1, Z2, Y1, Y2, SIB, DG = range(9)
TAB_Z, TAB_X = 9, 10
SLOTS = 9
M0, M1, SUB, SQ, TAB = range(5)

STEPS0 = [(0, 0), (0, 0), (0, 0), (0, 1), (0, 3), (1, 3), (0, 5), (7, 5), (0, 0), (7, 6), (0, 6), (1, 4), (2, 3), (0, 2), (0, 4), (0, 8)]
STEPS1 = [(0, 0), (0, 0), (0, 7), (0, 1), (0, 3), (1, 3), (0, 5), (7, 5), (0, 0), (0, 0), (0, 6), (1, 4), (2, 3), (0, 2), (0, 4), (0, 8)]
COL_STEPS = (2, 6, 7, 9, 10)
N_STEPS = 16


def pick(index, values):
    result = values[-1]
    for position in range(len(values) - 2, -1, -1):
        result = jnp.where(index == position, values[position], result)
    return result


def item_kernel(hist, basis, row_table, col_table, out, X, B, Q, T, ACC, RET, STA, STB,
                in_sem, send_sem, recv_sem, back_send, back_recv):
    r = lax.axis_index("row")
    c = lax.axis_index("col")
    z, x, y, k = r // 4, lax.rem(r, 4), c // 2, lax.rem(c, 2)
    s = 1 - 2 * k

    def row_at(dx, dz):
        return lax.rem(z + s * dz + 8, 4) * 4 + lax.rem(x + s * dx + 8, 4)

    def col_at(dy):
        return lax.rem(y + s * dy + 8, 4) * 2 + k

    def on_row(dx, dz):
        return (row_at(dx, dz), c)

    def on_col(dy):
        return (r, col_at(dy))

    sibling = (r, y * 2 + 1 - k)
    cross = (r, lax.rem(y + s + 4, 4) * 2 + 1 - k)
    sib_owner_col = jnp.where(k == 0, cross[1], sibling[1])

    peers = [on_row(1, 0), on_row(-1, 0), on_row(2, 0), on_row(0, 1), on_row(0, -1), on_row(0, 2),
             on_row(1, 1), on_row(-1, -1), on_col(1), on_col(-1), on_col(2), sibling, cross]
    barrier = pltpu.get_barrier_semaphore()
    for peer in peers:
        pl.semaphore_signal(barrier, inc=1, device_id=peer, device_id_type=MESH)

    copies_in = [pltpu.make_async_copy(hist.at[b], X.at[OWN, b], in_sem.at[b]) for b in range(2)]
    copies_in.append(pltpu.make_async_copy(basis, B.at[OWN], in_sem.at[2]))
    for item in copies_in:
        item.start()

    ACC[...] = jnp.zeros_like(ACC)

    def load_table(i, carry):
        T[OWN, 2 * i] = row_table[0, 0, i]
        T[OWN, 2 * i + 1] = row_table[0, 1, i]
        return carry

    lax.fori_loop(0, 16, load_table, 0)

    def load_col(i, carry):
        T[OWN, 32 + 2 * i] = col_table[0, 0, i]
        T[OWN, 33 + 2 * i] = col_table[0, 1, i]
        return carry

    lax.fori_loop(0, 8, load_col, 0)

    for item in copies_in:
        item.wait()
    for b in range(2):
        values = X[OWN, b].astype(F32)
        Q[OWN, b:b + 1] = jnp.sum(values * values, axis=0, keepdims=True) * (-SCALE)

    pl.semaphore_wait(barrier, len(peers))

    def remote(src, dst, send, recv, device):
        return pltpu.make_async_remote_copy(src_ref=src, dst_ref=dst, send_sem=send, recv_sem=recv,
                                            device_id=device, device_id_type=MESH)

    def part(kind, slot):
        if kind in (M0, M1):
            return X.at[slot, kind]
        return {SUB: B, SQ: Q, TAB: T}[kind].at[slot]

    def copy(path, kind, src, dst, device):
        return remote(part(kind, src), part(kind, dst), send_sem.at[path, kind], recv_sem.at[dst, kind], device)

    def arrived(kind, slot):
        copy(0, kind, slot, slot, sibling).wait_recv()

    paths = [(0, OWN, X1, on_row(1, 0)), (1, OWN, Z1, on_row(0, 1)), (2, OWN, Y1, on_col(1)),
             (4, X1, X2, on_row(1, 0)), (5, Z1, Z2, on_row(0, 1)), (6, Y1, Y2, on_col(1))]
    small = (TAB, SQ, SUB)

    for kind in (TAB, SQ, SUB, M0, M1):
        for path in paths[:3]:
            copy(path[0], kind, *path[1:]).start()
        if kind == TAB:
            copy(9, TAB, OWN, TAB_Z, on_row(0, -1)).start()
            copy(10, TAB, OWN, TAB_X, on_row(-1, 0)).start()

        @pl.when(k == 0)
        def _():
            copy(3, kind, OWN, SIB, sibling).start()

    def row_of(slot):
        return pick(slot, [r, row_at(-1, 0), row_at(-2, 0), row_at(0, -1), row_at(0, -2), r, r, r, row_at(-1, -1)])

    def col_of(slot):
        return pick(slot, [c, c, c, c, c, col_at(-1), col_at(-2), sib_owner_col, c])

    def chosen(i, j, ki, kj):
        return jnp.maximum(T[i, kj], T[j, ki + 1]), jnp.maximum(T[i, kj + 1], T[j, ki])

    def stage_a():
        target, owner = 2 * row_at(0, 1), 2 * row_at(-1, 0)
        return jnp.maximum(T[X1, target], T[TAB_Z, owner + 1])

    def stage_b():
        target, owner = 2 * row_at(1, 0), 2 * row_at(0, -1)
        return jnp.maximum(T[Z1, target], T[TAB_X, owner + 1])

    first, second = pl.ds(0, F // 2), pl.ds(F // 2, F // 2)
    to_z, to_x = on_row(0, 1), on_row(1, 0)

    def diagonal_copies():
        return [
            copy(7, TAB, X1, DG, to_z),
            copy(7, SQ, X1, DG, to_z),
            copy(8, SUB, Z1, DG, to_x),
            remote(STA, X.at[DG, 0, first], send_sem.at[7, M0], recv_sem.at[DG, M0], to_z),
            remote(STB, X.at[DG, 0, second], send_sem.at[8, M1], recv_sem.at[DG, M1], to_x),
        ]

    owners = [None, on_row(-1, 0), on_row(-2, 0), on_row(0, -1), on_row(0, -2), on_col(-1), on_col(-2),
              (r, sib_owner_col), on_row(-1, -1)]

    def give_back(slot):
        return remote(ACC.at[slot], RET.at[slot - 1], back_send.at[slot - 1], back_recv.at[slot - 1], owners[slot])

    def step_body(step, carry):
        @pl.when(jnp.logical_and(step == 2, k == 1))
        def _():
            for kind in (TAB, SQ, SUB, M0, M1):
                arrived(kind, SIB)

        @pl.when(step == 3)
        def _():
            for slot in (X1, Z1, Y1):
                for kind in small:
                    arrived(kind, slot)
            arrived(TAB, TAB_Z)
            arrived(TAB, TAB_X)
            for kind in small:
                for path in paths[3:]:
                    copy(path[0], kind, *path[1:]).start()

                @pl.when(k == 1)
                def _():
                    copy(3, kind, Y1, SIB, sibling).start()
            for kind in (M0, M1):
                for slot, path in zip((X1, Z1, Y1), paths[3:]):
                    arrived(kind, slot)
                    copy(path[0], kind, *path[1:]).start()

                @pl.when(k == 1)
                def _():
                    copy(3, kind, Y1, SIB, sibling).start()

        @pl.when(jnp.logical_and(step == 7, k == 0))
        def _():
            for kind in (TAB, SQ, SUB, M0, M1):
                arrived(kind, SIB)

        @pl.when(step == 8)
        def _():
            STA[...] = jnp.where(stage_a() == 0, X[X1, 0, 0:F // 2], X[X1, 1, 0:F // 2])
            STB[...] = jnp.where(stage_b() == 0, X[Z1, 0, F // 2:F], X[Z1, 1, F // 2:F])
            for item in diagonal_copies():
                item.start()

        @pl.when(step == 9)
        def _():
            for kind in (TAB, SQ, SUB, M0, M1):
                arrived(kind, Y2)

        @pl.when(step == 11)
        def _():
            for slot in (Y1, Y2, SIB):
                give_back(slot).start()
            for slot in (X2, Z2):
                for kind in (TAB, SQ, SUB, M0, M1):
                    arrived(kind, slot)

        @pl.when(step == 15)
        def _():
            for slot in (X1, X2, Z1, Z2):
                give_back(slot).start()
            for item in diagonal_copies():
                item.wait_recv()

        i = pick(step, [jnp.where(k == 0, a[0], b[0]) if a != b else a[0] for a, b in zip(STEPS0, STEPS1)])
        j = pick(step, [jnp.where(k == 0, a[1], b[1]) if a != b else a[1] for a, b in zip(STEPS0, STEPS1)])
        west = x < 2
        i = jnp.where(jnp.logical_and(step == 13, jnp.logical_not(west)), X2, i)
        j = jnp.where(jnp.logical_and(step == 13, jnp.logical_not(west)), Z2, j)
        runs = step != 8
        runs = jnp.logical_and(runs, jnp.logical_or(step != 2, k == 1))
        runs = jnp.logical_and(runs, jnp.logical_or(step != 9, k == 0))
        runs = jnp.logical_and(runs, jnp.logical_or(step != 10, y < 2))
        runs = jnp.logical_and(runs, jnp.logical_or(step != 14, z < 2))

        @pl.when(runs)
        def _():
            along_col = step == COL_STEPS[0]
            for other in COL_STEPS[1:]:
                along_col = jnp.logical_or(along_col, step == other)
            ki = jnp.where(along_col, 32 + 2 * col_of(i), 2 * row_of(i))
            kj = jnp.where(along_col, 32 + 2 * col_of(j), 2 * row_of(j))
            bi, bj = chosen(i, j, ki, kj)
            diagonal = step < 2
            bi = jnp.where(diagonal, step, bi)
            bj = jnp.where(diagonal, step, bj)
            at = jnp.where(j == DG, 0, bj)
            left = jnp.where(bi == 0, X[i, 0], X[i, 1])
            right = jnp.where(at == 0, X[j, 0], X[j, 1])
            inner = lax.dot_general(left, right, TN, preferred_element_type=F32)
            left_squares = jnp.where(bi == 0, Q[i, 0:1], Q[i, 1:2])
            right_squares = jnp.where(bj == 0, Q[j, 0:1], Q[j, 1:2])
            squares = jnp.broadcast_to(left_squares, (8, BS)).T[:, 0:1] + right_squares
            kernel = jnp.exp2(jnp.minimum(inner * (2 * SCALE) + squares, 0.0)).astype(BF16)
            left_basis = jnp.where(bi == 0, B[i, 0], B[i, 1])
            right_basis = jnp.where(bj == 0, B[j, 0], B[j, 1])
            theirs = lax.dot_general(kernel, right_basis, NT, preferred_element_type=F32).T
            mine = jnp.dot(left_basis, kernel, preferred_element_type=F32)
            for b in range(2):
                ACC[i, b] += jnp.where(jnp.logical_and(bi == b, jnp.logical_not(diagonal)), theirs, 0.0)
                ACC[j, b] += jnp.where(bj == b, mine, 0.0)

        return carry

    lax.fori_loop(0, N_STEPS, step_body, 0)
    give_back(DG).start()

    for path in paths:
        for kind in (TAB, SQ, SUB, M0, M1):
            copy(path[0], kind, *path[1:]).wait_send()
    for kind in (TAB, SQ, SUB, M0, M1):
        copy(3, kind, OWN, SIB, sibling).wait_send()
    copy(9, TAB, OWN, TAB_Z, on_row(0, -1)).wait_send()
    copy(10, TAB, OWN, TAB_X, on_row(-1, 0)).wait_send()
    for item in diagonal_copies():
        item.wait_send()
    total = ACC[OWN]
    for slot in (Y1, Y2, SIB, X1, X2, Z1, Z2, DG):
        give_back(slot).wait()
        total = total + RET[slot - 1]
    out[...] = total


def body(histograms, basis, row_pairs, col_pairs):
    return pl.pallas_call(
        item_kernel,
        out_shape=jax.ShapeDtypeStruct((2, COLS, BS), F32),
        in_specs=[
            pl.BlockSpec(memory_space=pl.ANY),
            pl.BlockSpec(memory_space=pl.ANY),
            pl.BlockSpec(memory_space=pltpu.SMEM),
            pl.BlockSpec(memory_space=pltpu.SMEM),
        ],
        out_specs=pl.BlockSpec(memory_space=pltpu.VMEM),
        scratch_shapes=[
            pltpu.VMEM((SLOTS, 2, F, BS), BF16),
            pltpu.VMEM((SLOTS, 2, COLS, BS), BF16),
            pltpu.VMEM((SLOTS, 8, BS), F32),
            pltpu.SMEM((11, 48), jnp.int32),
            pltpu.VMEM((SLOTS, 2, COLS, BS), F32),
            pltpu.VMEM((SLOTS - 1, 2, COLS, BS), F32),
            pltpu.VMEM((F // 2, BS), BF16),
            pltpu.VMEM((F // 2, BS), BF16),
            pltpu.SemaphoreType.DMA((3,)),
            pltpu.SemaphoreType.DMA((11, 5)),
            pltpu.SemaphoreType.DMA((11, 5)),
            pltpu.SemaphoreType.DMA((SLOTS - 1,)),
            pltpu.SemaphoreType.DMA((SLOTS - 1,)),
        ],
        compiler_params=pltpu.CompilerParams(
            collective_id=0, has_side_effects=True, vmem_limit_bytes=56 * 1024 * 1024
        ),
    )(jnp.swapaxes(histograms, 1, 2), basis, jnp.swapaxes(row_pairs, 1, 2), jnp.swapaxes(col_pairs, 1, 2))


def solution(mesh):
    spec = P(("row", "col"), None, None)
    return jax.shard_map(body, mesh=mesh, in_specs=(spec,) * 4, out_specs=spec, check_vma=False)
```

time: 78.3 us -> 71.1 us (0.908)
  local copies, waits for them, and re-layouts: 8.12 us -> 1.59 us
    unnamed x4 -> x1, local copies, waits for them, and re-layouts: 8.12 us -> 1.59 us
where the time goes in v2:
time: 71.1 us; the launch traced here: 70.9 us
  Pallas kernels  69.3 us (97%)
  local copies, waits for them, and re-layouts  1.59 us (2%)
    pallas_call x1, Pallas kernels, body(): pl.pallas_call(item_kernel, out_shape=jax.ShapeDtypeStruct((2, COLS, BS),...  69.3 us
    unnamed x1, local copies, waits for them, and re-layouts  1.59 us

profile of v2, /device:TPU:0, one launch (start us, length us, event | category | flops | bytes accessed | tf_op | source)
XLA Modules:
  0.0 70.9 jit_solution(14105624525389286180)
XLA Ops:
  0.0 69.3 %shard_map.46 = f32[2,32,640]{2,1,0:T(8,128)} custom-call(bf16[2,672,640]{2,1,0:T(8,128)(2,1)} %bitcast.3, bf16[2,32,640]{2,1,0:T(8,128)(2,1)} %basis.1, s32[1,2,16]{2,1,0:T(2,128)} %bitcast.4, s32[1,2,8]{2,1,0:T(2,128)} %bitcast.5), custom_call_target="tpu_custom_call" | custom-call | tf_op jit(solution)/shard_map/pallas_call | solution.py:280
  69.3 1.6 %copy.6 = f32[2,32,640]{2,1,0:T(8,128)} copy(f32[2,32,640]{2,1,0:T(8,128)} %shard_map.46) | data formatting | bytes 327680

commit v3 on v2

--- a/solution.py
+++ b/solution.py
@@ -16,7 +16,7 @@
 BF16 = jnp.bfloat16
 
 OWN, X1, X2, Z1, Z2, Y1, Y2, SIB, DG = range(9)
-TAB_Z, TAB_X = 9, 10
+TAB_Z, TAB_X, TAB_D = 9, 10, 11
 SLOTS = 9
 M0, M1, SUB, SQ, TAB = range(5)
 
@@ -33,7 +33,7 @@
     return result
 
 
-def item_kernel(hist, basis, row_table, col_table, out, X, B, Q, T, ACC, RET, STA, STB,
+def item_kernel(hist, basis, row_table, col_table, out, X, B, Q, T, ACC, BACK, RET, STA, STB,
                 in_sem, send_sem, recv_sem, back_send, back_recv):
     r = lax.axis_index("row")
     c = lax.axis_index("col")
@@ -56,11 +56,10 @@
     cross = (r, lax.rem(y + s + 4, 4) * 2 + 1 - k)
     sib_owner_col = jnp.where(k == 0, cross[1], sibling[1])
 
-    peers = [on_row(1, 0), on_row(-1, 0), on_row(2, 0), on_row(0, 1), on_row(0, -1), on_row(0, 2),
-             on_row(1, 1), on_row(-1, -1), on_col(1), on_col(-1), on_col(2), sibling, cross]
     barrier = pltpu.get_barrier_semaphore()
-    for peer in peers:
-        pl.semaphore_signal(barrier, inc=1, device_id=peer, device_id_type=MESH)
+    sources = [on_row(-1, 0), on_row(0, -1), on_col(-1), sibling]
+    for source in sources:
+        pl.semaphore_signal(barrier, inc=1, device_id=source, device_id_type=MESH)
 
     copies_in = [pltpu.make_async_copy(hist.at[b], X.at[OWN, b], in_sem.at[b]) for b in range(2)]
     copies_in.append(pltpu.make_async_copy(basis, B.at[OWN], in_sem.at[2]))
@@ -89,7 +88,7 @@
         values = X[OWN, b].astype(F32)
         Q[OWN, b:b + 1] = jnp.sum(values * values, axis=0, keepdims=True) * (-SCALE)
 
-    pl.semaphore_wait(barrier, len(peers))
+    pl.semaphore_wait(barrier, len(sources))
 
     def remote(src, dst, send, recv, device):
         return pltpu.make_async_remote_copy(src_ref=src, dst_ref=dst, send_sem=send, recv_sem=recv,
@@ -113,9 +112,6 @@
     for kind in (TAB, SQ, SUB, M0, M1):
         for path in paths[:3]:
             copy(path[0], kind, *path[1:]).start()
-        if kind == TAB:
-            copy(9, TAB, OWN, TAB_Z, on_row(0, -1)).start()
-            copy(10, TAB, OWN, TAB_X, on_row(-1, 0)).start()
 
         @pl.when(k == 0)
         def _():
@@ -154,7 +150,18 @@
               (r, sib_owner_col), on_row(-1, -1)]
 
     def give_back(slot):
-        return remote(ACC.at[slot], RET.at[slot - 1], back_send.at[slot - 1], back_recv.at[slot - 1], owners[slot])
+        part = (slot - 1, 0) if slot == DG else slot - 1
+        return remote(BACK.at[part], RET.at[part], back_send.at[slot - 1], back_recv.at[slot - 1], owners[slot])
+
+    def table_back():
+        return remote(T.at[OWN], T.at[TAB_D], send_sem.at[7, M1], recv_sem.at[TAB_D, TAB], owners[DG])
+
+    def start_back(slot):
+        if slot == DG:
+            BACK[slot - 1, 0] = (ACC[slot, 0] + ACC[slot, 1]).astype(BF16)
+        else:
+            BACK[slot - 1] = ACC[slot].astype(BF16)
+        give_back(slot).start()
 
     def step_body(step, carry):
         @pl.when(jnp.logical_and(step == 2, k == 1))
@@ -167,8 +174,8 @@
             for slot in (X1, Z1, Y1):
                 for kind in small:
                     arrived(kind, slot)
-            arrived(TAB, TAB_Z)
-            arrived(TAB, TAB_X)
+            copy(9, TAB, OWN, TAB_Z, on_row(0, -1)).start()
+            copy(10, TAB, OWN, TAB_X, on_row(-1, 0)).start()
             for kind in small:
                 for path in paths[3:]:
                     copy(path[0], kind, *path[1:]).start()
@@ -192,8 +199,13 @@
 
         @pl.when(step == 8)
         def _():
+            arrived(TAB, TAB_Z)
+            arrived(TAB, TAB_X)
             STA[...] = jnp.where(stage_a() == 0, X[X1, 0, 0:F // 2], X[X1, 1, 0:F // 2])
             STB[...] = jnp.where(stage_b() == 0, X[Z1, 0, F // 2:F], X[Z1, 1, F // 2:F])
+            for path in paths[3:5]:
+                for kind in (M0, M1):
+                    copy(path[0], kind, *path[1:]).wait_send()
             for item in diagonal_copies():
                 item.start()
 
@@ -205,17 +217,22 @@
         @pl.when(step == 11)
         def _():
             for slot in (Y1, Y2, SIB):
-                give_back(slot).start()
+                start_back(slot)
             for slot in (X2, Z2):
                 for kind in (TAB, SQ, SUB, M0, M1):
                     arrived(kind, slot)
 
+        for ready, slot in ((12, X1), (13, Z1), (14, X2)):
+            @pl.when(step == ready)
+            def _():
+                start_back(slot)
+
         @pl.when(step == 15)
         def _():
-            for slot in (X1, X2, Z1, Z2):
-                give_back(slot).start()
+            start_back(Z2)
             for item in diagonal_copies():
                 item.wait_recv()
+            table_back().start()
 
         i = pick(step, [jnp.where(k == 0, a[0], b[0]) if a != b else a[0] for a, b in zip(STEPS0, STEPS1)])
         j = pick(step, [jnp.where(k == 0, a[1], b[1]) if a != b else a[1] for a, b in zip(STEPS0, STEPS1)])
@@ -258,22 +275,28 @@
         return carry
 
     lax.fori_loop(0, N_STEPS, step_body, 0)
-    give_back(DG).start()
-
+    start_back(DG)
+    total = [ACC[OWN, b] for b in range(2)]
+    for slot in (Y1, Y2, SIB, X1, Z1, X2, Z2):
+        give_back(slot).wait()
+        for b in range(2):
+            total[b] = total[b] + RET[slot - 1, b].astype(F32)
     for path in paths:
         for kind in (TAB, SQ, SUB, M0, M1):
-            copy(path[0], kind, *path[1:]).wait_send()
+            if kind not in (M0, M1) or path not in paths[3:5]:
+                copy(path[0], kind, *path[1:]).wait_send()
     for kind in (TAB, SQ, SUB, M0, M1):
         copy(3, kind, OWN, SIB, sibling).wait_send()
     copy(9, TAB, OWN, TAB_Z, on_row(0, -1)).wait_send()
     copy(10, TAB, OWN, TAB_X, on_row(-1, 0)).wait_send()
     for item in diagonal_copies():
         item.wait_send()
-    total = ACC[OWN]
-    for slot in (Y1, Y2, SIB, X1, X2, Z1, Z2, DG):
-        give_back(slot).wait()
-        total = total + RET[slot - 1]
-    out[...] = total
+    table_back().wait()
+    mine = jnp.maximum(T[OWN, 2 * row_at(1, 1)], T[TAB_D, 2 * r + 1])
+    give_back(DG).wait()
+    last = RET[DG - 1, 0].astype(F32)
+    for b in range(2):
+        out[b] = total[b] + jnp.where(mine == b, last, 0.0)
 
 
 def body(histograms, basis, row_pairs, col_pairs):
@@ -291,14 +314,15 @@
             pltpu.VMEM((SLOTS, 2, F, BS), BF16),
             pltpu.VMEM((SLOTS, 2, COLS, BS), BF16),
             pltpu.VMEM((SLOTS, 8, BS), F32),
-            pltpu.SMEM((11, 48), jnp.int32),
+            pltpu.SMEM((12, 48), jnp.int32),
             pltpu.VMEM((SLOTS, 2, COLS, BS), F32),
-            pltpu.VMEM((SLOTS - 1, 2, COLS, BS), F32),
+            pltpu.VMEM((SLOTS - 1, 2, COLS, BS), BF16),
+            pltpu.VMEM((SLOTS - 1, 2, COLS, BS), BF16),
             pltpu.VMEM((F // 2, BS), BF16),
             pltpu.VMEM((F // 2, BS), BF16),
             pltpu.SemaphoreType.DMA((3,)),
-            pltpu.SemaphoreType.DMA((11, 5)),
-            pltpu.SemaphoreType.DMA((11, 5)),
+            pltpu.SemaphoreType.DMA((12, 5)),
+            pltpu.SemaphoreType.DMA((12, 5)),
             pltpu.SemaphoreType.DMA((SLOTS - 1,)),
             pltpu.SemaphoreType.DMA((SLOTS - 1,)),
         ],

time: 71.1 us -> 67 us (0.942)
  Pallas kernels: 69.3 us -> 65.3 us
    pallas_call x1, Pallas kernels: 69.3 us -> 65.3 us  [body(): pl.pallas_call(item_kernel, out_shape=jax.ShapeDtypeStruct((2, COLS, BS),...]
where the time goes in v3:
time: 67 us; the launch traced here: 66.9 us
  Pallas kernels  65.3 us (97%)
  local copies, waits for them, and re-layouts  1.59 us (2%)
    pallas_call x1, Pallas kernels, body(): pl.pallas_call(item_kernel, out_shape=jax.ShapeDtypeStruct((2, COLS, BS),...  65.3 us
    unnamed x1, local copies, waits for them, and re-layouts  1.59 us

profile of v3, /device:TPU:0, one launch (start us, length us, event | category | flops | bytes accessed | tf_op | source)
XLA Modules:
  0.0 66.9 jit_solution(18132342004991068462)
XLA Ops:
  0.0 65.3 %shard_map.46 = f32[2,32,640]{2,1,0:T(8,128)} custom-call(bf16[2,672,640]{2,1,0:T(8,128)(2,1)} %bitcast.3, bf16[2,32,640]{2,1,0:T(8,128)(2,1)} %basis.1, s32[1,2,16]{2,1,0:T(2,128)} %bitcast.4, s32[1,2,8]{2,1,0:T(2,128)} %bitcast.5), custom_call_target="tpu_custom_call" | custom-call | tf_op jit(solution)/shard_map/pallas_call | solution.py:303
  65.3 1.6 %copy.6 = f32[2,32,640]{2,1,0:T(8,128)} copy(f32[2,32,640]{2,1,0:T(8,128)} %shard_map.46) | data formatting | bytes 327680

commit v4 on v3

v4 whole, which is shorter than its diff:
```python
import jax
import jax.numpy as jnp
from jax import lax
from jax.experimental import pallas as pl
from jax.experimental.pallas import tpu as pltpu
from jax.sharding import PartitionSpec as P

F = 672
BS = 640
COLS = 32
SCALE = 1.4426950408889634 / (0.09 * F)
MESH = pl.DeviceIdType.MESH
NT = (((1,), (1,)), ((), ()))
TN = (((0,), (0,)), ((), ()))
F32 = jnp.float32
BF16 = jnp.bfloat16

OWN, X1, X2, Z1, Z2, Y1, Y2, SIB, DG, YN = range(10)
TAB_Z, TAB_X, TAB_D, TAB_Y, TAB_S = range(10, 15)
SLOTS = 10
M0, M1, N0, N1, SUB, SQ, TAB = range(7)
BULK, SMALL = (M0, M1, N0, N1), (TAB, SQ, SUB)
CUT = 512

STEPS = [
    ((0, 0), (0, 0)),
    ((0, 1), (0, 3)),
    ((1, 3), (0, 5)),
    ((7, 5), (0, 7)),
    ((0, 6), (0, 0)),
]
COL_PAIRS = ((2, 1), (3, 0), (3, 1), (4, 0))
LAST_STEPS = [
    ((1, 4), (2, 3)),
    ((0, 2), (0, 4)),
]


def pick(index, values):
    result = values[-1]
    for position in range(len(values) - 2, -1, -1):
        result = jnp.where(index == position, values[position], result)
    return result


def item_kernel(hist, basis, row_table, col_table, out, X, B, Q, T, ACC, BACK, RET, STA, STB, STC, G,
                in_sem, send_sem, recv_sem, back_send, back_recv):
    r = lax.axis_index("row")
    c = lax.axis_index("col")
    z, x, y, k = r // 4, lax.rem(r, 4), c // 2, lax.rem(c, 2)
    s = 1 - 2 * k

    def row_at(dx, dz):
        return lax.rem(z + s * dz + 8, 4) * 4 + lax.rem(x + s * dx + 8, 4)

    def col_at(dy):
        return lax.rem(y + s * dy + 8, 4) * 2 + k

    def on_row(dx, dz):
        return (row_at(dx, dz), c)

    def on_col(dy):
        return (r, col_at(dy))

    sibling = (r, y * 2 + 1 - k)
    cross = (r, lax.rem(y + s + 4, 4) * 2 + 1 - k)
    sib_next_col = lax.rem(y + 2, 4) * 2 + 1 - k
    sib_owner_col = jnp.where(k == 0, cross[1], sibling[1])

    barrier = pltpu.get_barrier_semaphore()
    sources = [on_row(-1, 0), on_row(0, -1), on_col(-1), sibling]
    for source in sources:
        pl.semaphore_signal(barrier, inc=1, device_id=source, device_id_type=MESH)

    copies_in = [pltpu.make_async_copy(hist.at[b], X.at[OWN, b], in_sem.at[b]) for b in range(2)]
    copies_in.append(pltpu.make_async_copy(basis, B.at[OWN], in_sem.at[2]))
    for item in copies_in:
        item.start()

    ACC[...] = jnp.zeros_like(ACC)

    def load_table(i, carry):
        T[OWN, 2 * i] = row_table[0, 0, i]
        T[OWN, 2 * i + 1] = row_table[0, 1, i]
        return carry

    lax.fori_loop(0, 16, load_table, 0)

    def load_col(i, carry):
        T[OWN, 32 + 2 * i] = col_table[0, 0, i]
        T[OWN, 33 + 2 * i] = col_table[0, 1, i]
        return carry

    lax.fori_loop(0, 8, load_col, 0)

    for item in copies_in:
        item.wait()
    for b in range(2):
        values = X[OWN, b].astype(F32)
        Q[OWN, b:b + 1] = jnp.sum(values * values, axis=0, keepdims=True) * (-SCALE)

    pl.semaphore_wait(barrier, len(sources))

    def remote(src, dst, send, recv, device):
        return pltpu.make_async_remote_copy(src_ref=src, dst_ref=dst, send_sem=send, recv_sem=recv,
                                            device_id=device, device_id_type=MESH)

    def part(kind, slot):
        if kind in BULK:
            return X.at[slot, kind % 2, pl.ds(0, CUT) if kind < 2 else pl.ds(CUT, F - CUT)]
        return {SUB: B, SQ: Q, TAB: T}[kind].at[slot]

    def copy(path, kind, src, dst, device):
        return remote(part(kind, src), part(kind, dst), send_sem.at[path, kind], recv_sem.at[dst, kind], device)

    def arrived(kind, slot):
        copy(0, kind, slot, slot, sibling).wait_recv()

    paths = [(0, OWN, X1, on_row(1, 0)), (1, OWN, Z1, on_row(0, 1)), (2, OWN, Y1, on_col(1)),
             (4, X1, X2, on_row(1, 0)), (5, Z1, Z2, on_row(0, 1)), (6, Y1, Y2, on_col(1))]

    def send_own(kind):
        for path in paths[:3]:
            copy(path[0], kind, *path[1:]).start()

        @pl.when(k == 0)
        def _():
            copy(3, kind, OWN, SIB, sibling).start()

    for kind in SMALL + (M0,):
        send_own(kind)

    def row_of(slot):
        return pick(slot, [r, row_at(-1, 0), row_at(-2, 0), row_at(0, -1), row_at(0, -2), r, r, r, row_at(-1, -1), r])

    def col_of(slot):
        return pick(slot, [c, c, c, c, c, col_at(-1), col_at(-2), sib_owner_col, c, col_at(1)])

    def chosen(i, j, ki, kj):
        return jnp.maximum(T[i, kj], T[j, ki + 1]), jnp.maximum(T[i, kj + 1], T[j, ki])

    def stage_a():
        target, owner = 2 * row_at(0, 1), 2 * row_at(-1, 0)
        return jnp.maximum(T[X1, target], T[TAB_Z, owner + 1])

    def stage_b():
        target, owner = 2 * row_at(1, 0), 2 * row_at(0, -1)
        return jnp.maximum(T[Z1, target], T[TAB_X, owner + 1])

    def stage_cross():
        return jnp.maximum(T[Y1, 32 + 2 * sib_next_col], T[TAB_S, 33 + 2 * col_at(-1)])

    def stage_far():
        return jnp.maximum(T[Y1, 32 + 2 * col_at(1)], T[TAB_Y, 33 + 2 * col_at(-1)])

    def stage_back():
        return jnp.maximum(T[OWN, 32 + 2 * col_at(-2)], T[Y2, 33 + 2 * c])

    def second_y():
        return remote(STC.at[0], X.at[Y2, 0], send_sem.at[6, M0], recv_sem.at[Y2, M0], on_col(1))

    def next_y():
        return [copy(13, kind, OWN, YN, on_col(-1)) for kind in SMALL] + [
            remote(STC.at[1], X.at[YN, 0], send_sem.at[13, M0], recv_sem.at[YN, M0], on_col(-1))]

    def sibling_table():
        return remote(T.at[Y2], T.at[TAB_S], send_sem.at[12, TAB], recv_sem.at[TAB_S, TAB], sibling)

    first, second = pl.ds(0, F // 2), pl.ds(F // 2, F // 2)
    to_z, to_x = on_row(0, 1), on_row(1, 0)

    def diagonal_copies():
        return [
            copy(7, TAB, X1, DG, to_z),
            copy(7, SQ, X1, DG, to_z),
            copy(8, SUB, Z1, DG, to_x),
            remote(STA, X.at[DG, 0, first], send_sem.at[7, M0], recv_sem.at[DG, M0], to_z),
            remote(STB, X.at[DG, 0, second], send_sem.at[8, M1], recv_sem.at[DG, M1], to_x),
        ]

    owners = [None, on_row(-1, 0), on_row(-2, 0), on_row(0, -1), on_row(0, -2), on_col(-1), on_col(-2),
              (r, sib_owner_col), on_row(-1, -1), on_col(1)]

    def give_back(slot):
        part = (slot - 1, 0) if slot == DG else slot - 1
        return remote(BACK.at[part], RET.at[part], back_send.at[slot - 1], back_recv.at[slot - 1], owners[slot])

    def table_back():
        return remote(T.at[OWN], T.at[TAB_D], send_sem.at[7, M1], recv_sem.at[TAB_D, TAB], owners[DG])

    def start_back(slot):
        BACK[slot - 1] = ACC[slot].astype(BF16)
        give_back(slot).start()

    west = x < 2

    def takes(dy):
        return ((z < 2) == (lax.rem(y + s * dy + 4, 4) < 2)) == (k == 1)

    takes_y, next_takes, last_takes = takes(0), takes(1), takes(-1)

    def pair_of(step, place):
        i, j = [pick(step, [entry[place][side] for entry in STEPS]) for side in range(2)]
        along_col = step < 0
        for s_col, p_col in COL_PAIRS:
            if p_col == place:
                along_col = jnp.logical_or(along_col, step == s_col)
        if place == 0:
            swap = jnp.logical_and(step == 4, k == 0)
            i, j = jnp.where(swap, Y1, i), jnp.where(swap, YN, j)
        else:
            swap = jnp.logical_and(step == 3, k == 0)
            i, j = jnp.where(swap, SIB, i), jnp.where(swap, Y2, j)
        ki = jnp.where(along_col, 32 + 2 * col_of(i), 2 * row_of(i))
        kj = jnp.where(along_col, 32 + 2 * col_of(j), 2 * row_of(j))
        bi, bj = chosen(i, j, ki, kj)
        diagonal = step == 0
        bi, bj = jnp.where(diagonal, place, bi), jnp.where(diagonal, place, bj)
        if place == 1:
            bi, bj = jnp.where(step == 4, -1, bi), jnp.where(step == 4, -1, bj)
        at = jnp.where(jnp.logical_or(j == Y2, j == YN), 0, bj)
        return i, j, bi, bj, at

    def last_pair_of(step, place):
        i, j = [pick(step, [entry[place][side] for entry in LAST_STEPS]) for side in range(2)]
        if place == 0:
            swap = jnp.logical_and(step == 1, jnp.logical_not(west))
            i, j = jnp.where(swap, X2, i), jnp.where(swap, Z2, j)
        bi, bj = chosen(i, j, 2 * row_of(i), 2 * row_of(j))
        if place == 1:
            left_out = jnp.logical_and(step == 1, takes_y)
            bi, bj = jnp.where(left_out, -1, bi), jnp.where(left_out, -1, bj)
        return i, j, bi, bj, bj

    def inner_of(i, j, bi, at, rows):
        left = jnp.where(bi == 0, X[i, 0, rows], X[i, 1, rows])
        right = X[j, at, rows] if isinstance(at, int) else jnp.where(at == 0, X[j, 0, rows], X[j, 1, rows])
        return lax.dot_general(left, right, TN, preferred_element_type=F32)

    def kernel_of(inner, i, j, bi, bj):
        left_squares = jnp.where(bi == 0, Q[i, 0:1], Q[i, 1:2])
        right_squares = jnp.where(bj == 0, Q[j, 0:1], Q[j, 1:2])
        squares = jnp.broadcast_to(left_squares, (8, BS)).T[:, 0:1] + right_squares
        return jnp.exp2(jnp.minimum(inner * (2 * SCALE) + squares, 0.0)).astype(BF16)

    def tile(i, j, bi, bj, at):
        return kernel_of(inner_of(i, j, bi, at, slice(None)), i, j, bi, bj)

    def add_terms(pairs, kernels, diagonal):
        for (i, j, bi, bj, _), kernel in zip(pairs, kernels):
            for_left, for_right = left_part(kernel, j, bj), right_part(kernel, i, bi)
            for b in range(2):
                ACC[i, b] += jnp.where(jnp.logical_and(bi == b, jnp.logical_not(diagonal)), for_left, 0.0)
                ACC[j, b] += jnp.where(bj == b, for_right, 0.0)

    def left_part(kernel, j, bj):
        right_basis = jnp.where(bj == 0, B[j, 0], B[j, 1])
        return lax.dot_general(kernel, right_basis, NT, preferred_element_type=F32).T

    def right_part(kernel, i, bi):
        return jnp.dot(jnp.where(bi == 0, B[i, 0], B[i, 1]), kernel, preferred_element_type=F32)

    def step_body(step, carry):
        @pl.when(step == 1)
        def _():
            for slot in (X1, Z1, Y1):
                for kind in SMALL:
                    arrived(kind, slot)
            copy(9, TAB, OWN, TAB_Z, on_row(0, -1)).start()
            copy(10, TAB, OWN, TAB_X, on_row(-1, 0)).start()
            copy(11, TAB, OWN, TAB_Y, on_col(-1)).start()
            for kind in SMALL:
                for path in paths[3:]:
                    copy(path[0], kind, *path[1:]).start()

                @pl.when(k == 1)
                def _():
                    copy(3, kind, Y1, SIB, sibling).start()

            for kind in BULK[1:]:
                send_own(kind)

            @pl.when(k == 1)
            def _():
                arrived(TAB, Y2)
                sibling_table().start()

            for kind in BULK:
                for slot, path in zip((X1, Z1), paths[3:]):
                    arrived(kind, slot)
                    copy(path[0], kind, *path[1:]).start()
                arrived(kind, Y1)

                @pl.when(k == 1)
                def _():
                    copy(3, kind, Y1, SIB, sibling).start()
            arrived(TAB, TAB_Y)

            @pl.when(k == 0)
            def _():
                arrived(TAB, TAB_S)
                STC[0] = jnp.where(stage_cross() == 0, X[Y1, 0], X[Y1, 1])
                second_y().start()

            @pl.when(k == 0)
            def _():
                arrived(TAB, Y2)

            @pl.when(jnp.logical_and(k == 0, last_takes))
            def _():
                STC[1] = jnp.where(stage_back() == 0, X[OWN, 0], X[OWN, 1])
                for item in next_y():
                    item.start()

            @pl.when(jnp.logical_and(k == 1, next_takes))
            def _():
                STC[0] = jnp.where(stage_far() == 0, X[Y1, 0], X[Y1, 1])
                second_y().start()

            arrived(TAB, TAB_Z)
            arrived(TAB, TAB_X)
            STA[...] = jnp.where(stage_a() == 0, X[X1, 0, 0:F // 2], X[X1, 1, 0:F // 2])
            STB[...] = jnp.where(stage_b() == 0, X[Z1, 0, F // 2:F], X[Z1, 1, F // 2:F])
            for item in diagonal_copies():
                item.start()

        @pl.when(step == 3)
        def _():
            arrived(TAB, X2)
            table_back().start()
            for kind in SMALL + BULK:
                arrived(kind, SIB)

            @pl.when(k == 0)
            def _():
                second_y().wait_recv()

            for kind in (SQ, SUB):
                arrived(kind, Y2)

        @pl.when(jnp.logical_and(step == 4, k == 0))
        def _():
            for item in next_y():
                item.wait_recv()

        @pl.when(jnp.logical_and(step == 4, k == 1))
        def _():
            second_y().wait_recv()

        pairs = [pair_of(step, place) for place in range(2)]
        add_terms(pairs, [tile(*pair) for pair in pairs], step == 0)
        return carry

    lax.fori_loop(0, len(STEPS) - 1 + takes_y.astype(jnp.int32), step_body, 0)
    for slot in (Y1, SIB, Y2):
        start_back(slot)

    @pl.when(jnp.logical_and(k == 0, takes_y))
    def _():
        start_back(YN)

    for slot, kinds in ((X2, (SQ, SUB, M0, M1)), (Z2, SMALL + (M0, M1))):
        for kind in kinds:
            arrived(kind, slot)
    head, rest = slice(0, CUT), slice(CUT, F)

    def early_body(step, carry):
        for place in range(2):
            i, j, bi, _, at = last_pair_of(step, place)
            G[2 * step + place] = inner_of(i, j, bi, at, head)
        return carry

    lax.fori_loop(0, len(LAST_STEPS), early_body, 0)
    for kind in (N0, N1):
        for slot in (X2, Z2):
            arrived(kind, slot)

    def last_body(step, carry):
        pairs = [last_pair_of(step, place) for place in range(2)]
        kernels = []
        for place, (i, j, bi, bj, at) in enumerate(pairs):
            kernels.append(kernel_of(G[2 * step + place] + inner_of(i, j, bi, at, rest), i, j, bi, bj))
        add_terms(pairs, kernels, False)

        @pl.when(step == 0)
        def _():
            start_back(X1)
            start_back(Z1)

        return carry

    lax.fori_loop(0, len(LAST_STEPS), last_body, 0)
    start_back(X2)
    start_back(Z2)
    for item in diagonal_copies():
        item.wait_recv()
    bi, bj = chosen(OWN, DG, 2 * r, 2 * row_at(-1, -1))
    kernel = tile(OWN, DG, bi, bj, 0)
    BACK[DG - 1, 0] = jnp.where(bj >= 0, right_part(kernel, OWN, bi), 0.0).astype(BF16)
    give_back(DG).start()
    for_left = left_part(kernel, DG, bj)
    total = [ACC[OWN, b] + jnp.where(bi == b, for_left, 0.0) for b in range(2)]

    for path in paths:
        for kind in SMALL if path[0] == 6 else SMALL + BULK:
            copy(path[0], kind, *path[1:]).wait_send()

    @pl.when(jnp.logical_or(k == 0, next_takes))
    def _():
        second_y().wait_send()

    @pl.when(jnp.logical_and(k == 0, last_takes))
    def _():
        for item in next_y():
            item.wait_send()

    @pl.when(k == 1)
    def _():
        sibling_table().wait_send()

    for kind in SMALL + BULK:
        copy(3, kind, OWN, SIB, sibling).wait_send()
    copy(9, TAB, OWN, TAB_Z, on_row(0, -1)).wait_send()
    copy(10, TAB, OWN, TAB_X, on_row(-1, 0)).wait_send()
    copy(11, TAB, OWN, TAB_Y, on_col(-1)).wait_send()
    for item in diagonal_copies():
        item.wait_send()
    for slot in (Y1, X1, Z1, X2, SIB, Y2, Z2):
        give_back(slot).wait()
        for b in range(2):
            total[b] = total[b] + RET[slot - 1, b].astype(F32)

    @pl.when(jnp.logical_and(k == 0, takes_y))
    def _():
        give_back(YN).wait_send()

    given = jnp.logical_and(k == 0, last_takes)

    @pl.when(given)
    def _():
        give_back(YN).wait_recv()

    @pl.when(jnp.logical_not(given))
    def _():
        RET[YN - 1] = jnp.zeros((2, COLS, BS), BF16)

    total = [total[b] + RET[YN - 1, b].astype(F32) for b in range(2)]
    table_back().wait()
    mine = jnp.maximum(T[OWN, 2 * row_at(1, 1)], T[TAB_D, 2 * r + 1])
    give_back(DG).wait()
    last = RET[DG - 1, 0].astype(F32)
    for b in range(2):
        out[b] = total[b] + jnp.where(mine == b, last, 0.0)


def body(histograms, basis, row_pairs, col_pairs):
    return pl.pallas_call(
        item_kernel,
        out_shape=jax.ShapeDtypeStruct((2, COLS, BS), F32),
        in_specs=[
            pl.BlockSpec(memory_space=pl.ANY),
            pl.BlockSpec(memory_space=pl.ANY),
            pl.BlockSpec(memory_space=pltpu.SMEM),
            pl.BlockSpec(memory_space=pltpu.SMEM),
        ],
        out_specs=pl.BlockSpec(memory_space=pltpu.VMEM),
        scratch_shapes=[
            pltpu.VMEM((SLOTS, 2, F, BS), BF16),
            pltpu.VMEM((SLOTS, 2, COLS, BS), BF16),
            pltpu.VMEM((SLOTS, 8, BS), F32),
            pltpu.SMEM((15, 48), jnp.int32),
            pltpu.VMEM((SLOTS, 2, COLS, BS), F32),
            pltpu.VMEM((SLOTS - 1, 2, COLS, BS), BF16),
            pltpu.VMEM((SLOTS - 1, 2, COLS, BS), BF16),
            pltpu.VMEM((F // 2, BS), BF16),
            pltpu.VMEM((F // 2, BS), BF16),
            pltpu.VMEM((2, F, BS), BF16),
            pltpu.VMEM((4, BS, BS), F32),
            pltpu.SemaphoreType.DMA((3,)),
            pltpu.SemaphoreType.DMA((15, 7)),
            pltpu.SemaphoreType.DMA((15, 7)),
            pltpu.SemaphoreType.DMA((SLOTS - 1,)),
            pltpu.SemaphoreType.DMA((SLOTS - 1,)),
        ],
        compiler_params=pltpu.CompilerParams(
            collective_id=0, has_side_effects=True, vmem_limit_bytes=56 * 1024 * 1024
        ),
    )(jnp.swapaxes(histograms, 1, 2), basis, jnp.swapaxes(row_pairs, 1, 2), jnp.swapaxes(col_pairs, 1, 2))


def solution(mesh):
    spec = P(("row", "col"), None, None)
    return jax.shard_map(body, mesh=mesh, in_specs=(spec,) * 4, out_specs=spec, check_vma=False)
```

time: 67 us -> 64.1 us (0.957)
  Pallas kernels: 65.3 us -> 62.4 us
    pallas_call x1, Pallas kernels: 65.3 us -> 62.4 us  [body(): pl.pallas_call(item_kernel, out_shape=jax.ShapeDtypeStruct((2, COLS, BS),...]
where the time goes in v4:
time: 64.1 us; the launch traced here: 64 us
  Pallas kernels  62.4 us (97%)
  local copies, waits for them, and re-layouts  1.59 us (2%)
    pallas_call x1, Pallas kernels, body(): pl.pallas_call(item_kernel, out_shape=jax.ShapeDtypeStruct((2, COLS, BS),...  62.4 us
    unnamed x1, local copies, waits for them, and re-layouts  1.59 us

profile of v4, /device:TPU:0, one launch (start us, length us, event | category | flops | bytes accessed | tf_op | source)
XLA Modules:
  0.0 64.0 jit_solution(1865422964501948079)
XLA Ops:
  0.0 62.4 %shard_map.46 = f32[2,32,640]{2,1,0:T(8,128)} custom-call(bf16[2,672,640]{2,1,0:T(8,128)(2,1)} %bitcast.3, bf16[2,32,640]{2,1,0:T(8,128)(2,1)} %basis.1, s32[1,2,16]{2,1,0:T(2,128)} %bitcast.4, s32[1,2,8]{2,1,0:T(2,128)} %bitcast.5), custom_call_target="tpu_custom_call" | custom-call | tf_op jit(solution)/shard_map/pallas_call | solution.py:457
  62.4 1.6 %copy.6 = f32[2,32,640]{2,1,0:T(8,128)} copy(f32[2,32,640]{2,1,0:T(8,128)} %shard_map.46) | data formatting | bytes 327680

commit v5 on v4

--- a/solution.py
+++ b/solution.py
@@ -20,6 +20,7 @@
 SLOTS = 10
 M0, M1, N0, N1, SUB, SQ, TAB = range(7)
 BULK, SMALL = (M0, M1, N0, N1), (TAB, SQ, SUB)
+HALF = 352
 CUT = 512
 
 STEPS = [
@@ -43,7 +44,7 @@
     return result
 
 
-def item_kernel(hist, basis, row_table, col_table, out, X, B, Q, T, ACC, BACK, RET, STA, STB, STC, G,
+def item_kernel(hist, basis, row_table, col_table, out, X, B, Q, T, ACC, BACK, RET, STA, STB, STC, STE, G,
                 in_sem, send_sem, recv_sem, back_send, back_recv):
     r = lax.axis_index("row")
     c = lax.axis_index("col")
@@ -127,7 +128,7 @@
         def _():
             copy(3, kind, OWN, SIB, sibling).start()
 
-    for kind in SMALL + (M0,):
+    for kind in SMALL + (M0, M1):
         send_own(kind)
 
     def row_of(slot):
@@ -166,14 +167,14 @@
     def sibling_table():
         return remote(T.at[Y2], T.at[TAB_S], send_sem.at[12, TAB], recv_sem.at[TAB_S, TAB], sibling)
 
-    first, second = pl.ds(0, F // 2), pl.ds(F // 2, F // 2)
+    first, second = pl.ds(0, HALF), pl.ds(HALF, F - HALF)
     to_z, to_x = on_row(0, 1), on_row(1, 0)
 
     def diagonal_copies():
         return [
             copy(7, TAB, X1, DG, to_z),
             copy(7, SQ, X1, DG, to_z),
-            copy(8, SUB, Z1, DG, to_x),
+            remote(STE, B.at[DG, 0], send_sem.at[8, SUB], recv_sem.at[DG, SUB], to_x),
             remote(STA, X.at[DG, 0, first], send_sem.at[7, M0], recv_sem.at[DG, M0], to_z),
             remote(STB, X.at[DG, 0, second], send_sem.at[8, M1], recv_sem.at[DG, M1], to_x),
         ]
@@ -261,7 +262,7 @@
         return jnp.dot(jnp.where(bi == 0, B[i, 0], B[i, 1]), kernel, preferred_element_type=F32)
 
     def step_body(step, carry):
-        @pl.when(step == 1)
+        @pl.when(step == 0)
         def _():
             for slot in (X1, Z1, Y1):
                 for kind in SMALL:
@@ -277,7 +278,7 @@
                 def _():
                     copy(3, kind, Y1, SIB, sibling).start()
 
-            for kind in BULK[1:]:
+            for kind in BULK[2:]:
                 send_own(kind)
 
             @pl.when(k == 1)
@@ -319,8 +320,9 @@
 
             arrived(TAB, TAB_Z)
             arrived(TAB, TAB_X)
-            STA[...] = jnp.where(stage_a() == 0, X[X1, 0, 0:F // 2], X[X1, 1, 0:F // 2])
-            STB[...] = jnp.where(stage_b() == 0, X[Z1, 0, F // 2:F], X[Z1, 1, F // 2:F])
+            STA[...] = jnp.where(stage_a() == 0, X[X1, 0, 0:HALF], X[X1, 1, 0:HALF])
+            STB[...] = jnp.where(stage_b() == 0, X[Z1, 0, HALF:F], X[Z1, 1, HALF:F])
+            STE[...] = jnp.where(stage_b() == 0, B[Z1, 0], B[Z1, 1])
             for item in diagonal_copies():
                 item.start()
 
@@ -398,7 +400,7 @@
     kernel = tile(OWN, DG, bi, bj, 0)
     BACK[DG - 1, 0] = jnp.where(bj >= 0, right_part(kernel, OWN, bi), 0.0).astype(BF16)
     give_back(DG).start()
-    for_left = left_part(kernel, DG, bj)
+    for_left = left_part(kernel, DG, 0)
     total = [ACC[OWN, b] + jnp.where(bi == b, for_left, 0.0) for b in range(2)]
 
     for path in paths:
@@ -467,14 +469,15 @@
         scratch_shapes=[
             pltpu.VMEM((SLOTS, 2, F, BS), BF16),
             pltpu.VMEM((SLOTS, 2, COLS, BS), BF16),
-            pltpu.VMEM((SLOTS, 8, BS), F32),
+            pltpu.VMEM((SLOTS, 2, BS), F32),
             pltpu.SMEM((15, 48), jnp.int32),
             pltpu.VMEM((SLOTS, 2, COLS, BS), F32),
             pltpu.VMEM((SLOTS - 1, 2, COLS, BS), BF16),
             pltpu.VMEM((SLOTS - 1, 2, COLS, BS), BF16),
-            pltpu.VMEM((F // 2, BS), BF16),
-            pltpu.VMEM((F // 2, BS), BF16),
+            pltpu.VMEM((HALF, BS), BF16),
+            pltpu.VMEM((F - HALF, BS), BF16),
             pltpu.VMEM((2, F, BS), BF16),
+            pltpu.VMEM((COLS, BS), BF16),
             pltpu.VMEM((4, BS, BS), F32),
             pltpu.SemaphoreType.DMA((3,)),
             pltpu.SemaphoreType.DMA((15, 7)),

time: 64.1 us -> 63.6 us (level)
  no operation moved by 1% of the time
where the time goes in v5:
time: 63.6 us; the launch traced here: 63.4 us
  Pallas kernels  61.8 us (97%)
  local copies, waits for them, and re-layouts  1.59 us (2%)
    pallas_call x1, Pallas kernels, body(): pl.pallas_call(item_kernel, out_shape=jax.ShapeDtypeStruct((2, COLS, BS),...  61.8 us
    unnamed x1, local copies, waits for them, and re-layouts  1.59 us

profile of v5, /device:TPU:0, one launch (start us, length us, event | category | flops | bytes accessed | tf_op | source)
XLA Modules:
  0.0 63.4 jit_solution(11435534835175367459)
XLA Ops:
  0.0 61.8 %shard_map.46 = f32[2,32,640]{2,1,0:T(8,128)} custom-call(bf16[2,672,640]{2,1,0:T(8,128)(2,1)} %bitcast.3, bf16[2,32,640]{2,1,0:T(8,128)(2,1)} %basis.1, s32[1,2,16]{2,1,0:T(2,128)} %bitcast.4, s32[1,2,8]{2,1,0:T(2,128)} %bitcast.5), custom_call_target="tpu_custom_call" | custom-call | tf_op jit(solution)/shard_map/pallas_call | solution.py:459
  61.8 1.6 %copy.6 = f32[2,32,640]{2,1,0:T(8,128)} copy(f32[2,32,640]{2,1,0:T(8,128)} %shard_map.46) | data formatting | bytes 327680

commit v6 on v5

--- a/solution.py
+++ b/solution.py
@@ -18,8 +18,8 @@
 OWN, X1, X2, Z1, Z2, Y1, Y2, SIB, DG, YN = range(10)
 TAB_Z, TAB_X, TAB_D, TAB_Y, TAB_S = range(10, 15)
 SLOTS = 10
-M0, M1, N0, N1, SUB, SQ, TAB = range(7)
-BULK, SMALL = (M0, M1, N0, N1), (TAB, SQ, SUB)
+HEAD, REST, SUB, SQ, TAB = range(5)
+BULK, SMALL = (HEAD, REST), (TAB, SQ, SUB)
 HALF = 352
 CUT = 512
 
@@ -44,7 +44,7 @@
     return result
 
 
-def item_kernel(hist, basis, row_table, col_table, out, X, B, Q, T, ACC, BACK, RET, STA, STB, STC, STE, G,
+def item_kernel(hist, basis, row_table, col_table, out, X, B, Q, T, ACC, BACK, RET, STA, STB, STC, STE, G, RT, CT,
                 in_sem, send_sem, recv_sem, back_send, back_recv):
     r = lax.axis_index("row")
     c = lax.axis_index("col")
@@ -75,21 +75,25 @@
 
     copies_in = [pltpu.make_async_copy(hist.at[b], X.at[OWN, b], in_sem.at[b]) for b in range(2)]
     copies_in.append(pltpu.make_async_copy(basis, B.at[OWN], in_sem.at[2]))
-    for item in copies_in:
+    tables_in = [pltpu.make_async_copy(row_table, RT, in_sem.at[3]), pltpu.make_async_copy(col_table, CT, in_sem.at[4])]
+    for item in tables_in + copies_in:
         item.start()
 
     ACC[...] = jnp.zeros_like(ACC)
 
+    for item in tables_in:
+        item.wait()
+
     def load_table(i, carry):
-        T[OWN, 2 * i] = row_table[0, 0, i]
-        T[OWN, 2 * i + 1] = row_table[0, 1, i]
+        T[OWN, 2 * i] = RT[0, 0, i]
+        T[OWN, 2 * i + 1] = RT[0, 1, i]
         return carry
 
     lax.fori_loop(0, 16, load_table, 0)
 
     def load_col(i, carry):
-        T[OWN, 32 + 2 * i] = col_table[0, 0, i]
-        T[OWN, 33 + 2 * i] = col_table[0, 1, i]
+        T[OWN, 32 + 2 * i] = CT[0, 0, i]
+        T[OWN, 33 + 2 * i] = CT[0, 1, i]
         return carry
 
     lax.fori_loop(0, 8, load_col, 0)
@@ -108,7 +112,7 @@
 
     def part(kind, slot):
         if kind in BULK:
-            return X.at[slot, kind % 2, pl.ds(0, CUT) if kind < 2 else pl.ds(CUT, F - CUT)]
+            return X.at[slot, :, pl.ds(0, CUT) if kind == HEAD else pl.ds(CUT, F - CUT)]
         return {SUB: B, SQ: Q, TAB: T}[kind].at[slot]
 
     def copy(path, kind, src, dst, device):
@@ -128,7 +132,7 @@
         def _():
             copy(3, kind, OWN, SIB, sibling).start()
 
-    for kind in SMALL + (M0, M1):
+    for kind in SMALL + (HEAD,):
         send_own(kind)
 
     def row_of(slot):
@@ -158,11 +162,11 @@
         return jnp.maximum(T[OWN, 32 + 2 * col_at(-2)], T[Y2, 33 + 2 * c])
 
     def second_y():
-        return remote(STC.at[0], X.at[Y2, 0], send_sem.at[6, M0], recv_sem.at[Y2, M0], on_col(1))
+        return remote(STC.at[0], X.at[Y2, 0], send_sem.at[6, HEAD], recv_sem.at[Y2, HEAD], on_col(1))
 
     def next_y():
         return [copy(13, kind, OWN, YN, on_col(-1)) for kind in SMALL] + [
-            remote(STC.at[1], X.at[YN, 0], send_sem.at[13, M0], recv_sem.at[YN, M0], on_col(-1))]
+            remote(STC.at[1], X.at[YN, 0], send_sem.at[13, HEAD], recv_sem.at[YN, HEAD], on_col(-1))]
 
     def sibling_table():
         return remote(T.at[Y2], T.at[TAB_S], send_sem.at[12, TAB], recv_sem.at[TAB_S, TAB], sibling)
@@ -175,8 +179,8 @@
             copy(7, TAB, X1, DG, to_z),
             copy(7, SQ, X1, DG, to_z),
             remote(STE, B.at[DG, 0], send_sem.at[8, SUB], recv_sem.at[DG, SUB], to_x),
-            remote(STA, X.at[DG, 0, first], send_sem.at[7, M0], recv_sem.at[DG, M0], to_z),
-            remote(STB, X.at[DG, 0, second], send_sem.at[8, M1], recv_sem.at[DG, M1], to_x),
+            remote(STA, X.at[DG, 0, first], send_sem.at[7, HEAD], recv_sem.at[DG, HEAD], to_z),
+            remote(STB, X.at[DG, 0, second], send_sem.at[8, REST], recv_sem.at[DG, REST], to_x),
         ]
 
     owners = [None, on_row(-1, 0), on_row(-2, 0), on_row(0, -1), on_row(0, -2), on_col(-1), on_col(-2),
@@ -187,7 +191,7 @@
         return remote(BACK.at[part], RET.at[part], back_send.at[slot - 1], back_recv.at[slot - 1], owners[slot])
 
     def table_back():
-        return remote(T.at[OWN], T.at[TAB_D], send_sem.at[7, M1], recv_sem.at[TAB_D, TAB], owners[DG])
+        return remote(T.at[OWN], T.at[TAB_D], send_sem.at[7, REST], recv_sem.at[TAB_D, TAB], owners[DG])
 
     def start_back(slot):
         BACK[slot - 1] = ACC[slot].astype(BF16)
@@ -278,8 +282,7 @@
                 def _():
                     copy(3, kind, Y1, SIB, sibling).start()
 
-            for kind in BULK[2:]:
-                send_own(kind)
+            send_own(REST)
 
             @pl.when(k == 1)
             def _():
@@ -361,7 +364,7 @@
     def _():
         start_back(YN)
 
-    for slot, kinds in ((X2, (SQ, SUB, M0, M1)), (Z2, SMALL + (M0, M1))):
+    for slot, kinds in ((X2, (SQ, SUB, HEAD)), (Z2, SMALL + (HEAD,))):
         for kind in kinds:
             arrived(kind, slot)
     head, rest = slice(0, CUT), slice(CUT, F)
@@ -373,9 +376,8 @@
         return carry
 
     lax.fori_loop(0, len(LAST_STEPS), early_body, 0)
-    for kind in (N0, N1):
-        for slot in (X2, Z2):
-            arrived(kind, slot)
+    for slot in (X2, Z2):
+        arrived(REST, slot)
 
     def last_body(step, carry):
         pairs = [last_pair_of(step, place) for place in range(2)]
@@ -462,8 +464,8 @@
         in_specs=[
             pl.BlockSpec(memory_space=pl.ANY),
             pl.BlockSpec(memory_space=pl.ANY),
-            pl.BlockSpec(memory_space=pltpu.SMEM),
-            pl.BlockSpec(memory_space=pltpu.SMEM),
+            pl.BlockSpec(memory_space=pl.ANY),
+            pl.BlockSpec(memory_space=pl.ANY),
         ],
         out_specs=pl.BlockSpec(memory_space=pltpu.VMEM),
         scratch_shapes=[
@@ -479,9 +481,11 @@
             pltpu.VMEM((2, F, BS), BF16),
             pltpu.VMEM((COLS, BS), BF16),
             pltpu.VMEM((4, BS, BS), F32),
-            pltpu.SemaphoreType.DMA((3,)),
-            pltpu.SemaphoreType.DMA((15, 7)),
-            pltpu.SemaphoreType.DMA((15, 7)),
+            pltpu.SMEM((1, 2, 16), jnp.int32),
+            pltpu.SMEM((1, 2, 8), jnp.int32),
+            pltpu.SemaphoreType.DMA((5,)),
+            pltpu.SemaphoreType.DMA((15, 5)),
+            pltpu.SemaphoreType.DMA((15, 5)),
             pltpu.SemaphoreType.DMA((SLOTS - 1,)),
             pltpu.SemaphoreType.DMA((SLOTS - 1,)),
         ],

time: 63.6 us -> 62.3 us (0.980)
  Pallas kernels: 61.8 us -> 60.5 us
    pallas_call x1, Pallas kernels: 61.8 us -> 60.5 us  [body(): pl.pallas_call(item_kernel, out_shape=jax.ShapeDtypeStruct((2, COLS, BS),...]
where the time goes in v6:
time: 62.3 us; the launch traced here: 62.1 us
  Pallas kernels  60.5 us (97%)
  local copies, waits for them, and re-layouts  1.59 us (3%)
    pallas_call x1, Pallas kernels, body(): pl.pallas_call(item_kernel, out_shape=jax.ShapeDtypeStruct((2, COLS, BS),...  60.5 us
    unnamed x1, local copies, waits for them, and re-layouts  1.59 us

profile of v6, /device:TPU:0, one launch (start us, length us, event | category | flops | bytes accessed | tf_op | source)
XLA Modules:
  0.0 62.1 jit_solution(1572784861001889768)
XLA Ops:
  0.0 60.5 %shard_map.46 = f32[2,32,640]{2,1,0:T(8,128)} custom-call(bf16[2,672,640]{2,1,0:T(8,128)(2,1)} %bitcast.3, bf16[2,32,640]{2,1,0:T(8,128)(2,1)} %basis.1, s32[1,2,16]{2,1,0:T(2,128)} %bitcast.4, s32[1,2,8]{2,1,0:T(2,128)} %bitcast.5), custom_call_target="tpu_custom_call" | custom-call | tf_op jit(solution)/shard_map/pallas_call | solution.py:461
  60.5 1.6 %copy.6 = f32[2,32,640]{2,1,0:T(8,128)} copy(f32[2,32,640]{2,1,0:T(8,128)} %shard_map.46) | data formatting | bytes 327680

commit v7 on v6

--- a/solution.py
+++ b/solution.py
@@ -171,7 +171,6 @@
     def sibling_table():
         return remote(T.at[Y2], T.at[TAB_S], send_sem.at[12, TAB], recv_sem.at[TAB_S, TAB], sibling)
 
-    first, second = pl.ds(0, HALF), pl.ds(HALF, F - HALF)
     to_z, to_x = on_row(0, 1), on_row(1, 0)
 
     def diagonal_copies():
@@ -179,8 +178,10 @@
             copy(7, TAB, X1, DG, to_z),
             copy(7, SQ, X1, DG, to_z),
             remote(STE, B.at[DG, 0], send_sem.at[8, SUB], recv_sem.at[DG, SUB], to_x),
-            remote(STA, X.at[DG, 0, first], send_sem.at[7, HEAD], recv_sem.at[DG, HEAD], to_z),
-            remote(STB, X.at[DG, 0, second], send_sem.at[8, REST], recv_sem.at[DG, REST], to_x),
+            remote(STA.at[pl.ds(0, 256)], X.at[DG, 0, pl.ds(0, 256)], send_sem.at[7, HEAD], recv_sem.at[DG, HEAD], to_z),
+            remote(STB.at[pl.ds(64, 256)], X.at[DG, 0, pl.ds(416, 256)], send_sem.at[8, REST], recv_sem.at[DG, REST], to_x),
+            remote(STA.at[pl.ds(256, 96)], X.at[DG, 0, pl.ds(256, 96)], send_sem.at[14, HEAD], recv_sem.at[TAB_Z, HEAD], to_z),
+            remote(STB.at[pl.ds(0, 64)], X.at[DG, 0, pl.ds(352, 64)], send_sem.at[14, REST], recv_sem.at[TAB_Z, REST], to_x),
         ]
 
     owners = [None, on_row(-1, 0), on_row(-2, 0), on_row(0, -1), on_row(0, -2), on_col(-1), on_col(-2),
@@ -359,6 +360,28 @@
     lax.fori_loop(0, len(STEPS) - 1 + takes_y.astype(jnp.int32), step_body, 0)
     for slot in (Y1, SIB, Y2):
         start_back(slot)
+    for path in paths:
+        for kind in SMALL if path[0] >= 4 else SMALL + BULK:
+            copy(path[0], kind, *path[1:]).wait_send()
+
+    @pl.when(jnp.logical_or(k == 0, next_takes))
+    def _():
+        second_y().wait_send()
+
+    @pl.when(jnp.logical_and(k == 0, last_takes))
+    def _():
+        for item in next_y():
+            item.wait_send()
+
+    @pl.when(k == 1)
+    def _():
+        sibling_table().wait_send()
+
+    for kind in SMALL + BULK:
+        copy(3, kind, OWN, SIB, sibling).wait_send()
+    copy(9, TAB, OWN, TAB_Z, on_row(0, -1)).wait_send()
+    copy(10, TAB, OWN, TAB_X, on_row(-1, 0)).wait_send()
+    copy(11, TAB, OWN, TAB_Y, on_col(-1)).wait_send()
 
     @pl.when(jnp.logical_and(k == 0, takes_y))
     def _():
@@ -396,37 +419,22 @@
     lax.fori_loop(0, len(LAST_STEPS), last_body, 0)
     start_back(X2)
     start_back(Z2)
-    for item in diagonal_copies():
+    diagonal_parts = diagonal_copies()
+    for item in diagonal_parts[:-2]:
         item.wait_recv()
     bi, bj = chosen(OWN, DG, 2 * r, 2 * row_at(-1, -1))
-    kernel = tile(OWN, DG, bi, bj, 0)
+    G[0] = inner_of(OWN, DG, bi, 0, slice(0, 256)) + inner_of(OWN, DG, bi, 0, slice(416, F))
+    for item in diagonal_parts[-2:]:
+        item.wait_recv()
+    kernel = kernel_of(G[0] + inner_of(OWN, DG, bi, 0, slice(256, 416)), OWN, DG, bi, bj)
     BACK[DG - 1, 0] = jnp.where(bj >= 0, right_part(kernel, OWN, bi), 0.0).astype(BF16)
     give_back(DG).start()
     for_left = left_part(kernel, DG, 0)
     total = [ACC[OWN, b] + jnp.where(bi == b, for_left, 0.0) for b in range(2)]
 
-    for path in paths:
-        for kind in SMALL if path[0] == 6 else SMALL + BULK:
+    for path in paths[3:5]:
+        for kind in BULK:
             copy(path[0], kind, *path[1:]).wait_send()
-
-    @pl.when(jnp.logical_or(k == 0, next_takes))
-    def _():
-        second_y().wait_send()
-
-    @pl.when(jnp.logical_and(k == 0, last_takes))
-    def _():
-        for item in next_y():
-            item.wait_send()
-
-    @pl.when(k == 1)
-    def _():
-        sibling_table().wait_send()
-
-    for kind in SMALL + BULK:
-        copy(3, kind, OWN, SIB, sibling).wait_send()
-    copy(9, TAB, OWN, TAB_Z, on_row(0, -1)).wait_send()
-    copy(10, TAB, OWN, TAB_X, on_row(-1, 0)).wait_send()
-    copy(11, TAB, OWN, TAB_Y, on_col(-1)).wait_send()
     for item in diagonal_copies():
         item.wait_send()
     for slot in (Y1, X1, Z1, X2, SIB, Y2, Z2):

time: 62.3 us -> 62.4 us (level)
  no operation moved by 1% of the time
where the time goes in v7:
time: 62.4 us; the launch traced here: 62.2 us
  Pallas kernels  60.6 us (97%)
  local copies, waits for them, and re-layouts  1.59 us (3%)
    pallas_call x1, Pallas kernels, body(): pl.pallas_call(item_kernel, out_shape=jax.ShapeDtypeStruct((2, COLS, BS),...  60.6 us
    unnamed x1, local copies, waits for them, and re-layouts  1.59 us

profile of v7, /device:TPU:0, one launch (start us, length us, event | category | flops | bytes accessed | tf_op | source)
XLA Modules:
  0.0 62.2 jit_solution(7707811105128754349)
XLA Ops:
  0.0 60.6 %shard_map.46 = f32[2,32,640]{2,1,0:T(8,128)} custom-call(bf16[2,672,640]{2,1,0:T(8,128)(2,1)} %bitcast.3, bf16[2,32,640]{2,1,0:T(8,128)(2,1)} %basis.1, s32[1,2,16]{2,1,0:T(2,128)} %bitcast.4, s32[1,2,8]{2,1,0:T(2,128)} %bitcast.5), custom_call_target="tpu_custom_call" | custom-call | tf_op jit(solution)/shard_map/pallas_call | solution.py:469
  60.6 1.6 %copy.6 = f32[2,32,640]{2,1,0:T(8,128)} copy(f32[2,32,640]{2,1,0:T(8,128)} %shard_map.46) | data formatting | bytes 327680
